TPU v7x, 256 devices: a whole 4x4x8 slice. The times are simulated.
256 devices in a mesh: resp: 16 (over y, z_hi), ctx: 16 (over x, z_lo, core).
Axes of the slice: x: 4, y: 4, z: 8 (z_hi: 4, z_lo: 2; z = z_hi * 2 + z_lo), core: 2. Of those that a mesh axis runs over, the one named last changes fastest.
Arguments:
- queries: bfloat16 [16, 2048, 2560], P('resp', 'ctx'), may hold values from -96 to 96
- resp_keys: bfloat16 [16, 2048, 512], P('resp', 'ctx'), may hold values from -6 to 6
- resp_values: bfloat16 [16, 2048, 512], P('resp', 'ctx'), may hold values from -6 to 6
- prompt_keys: bfloat16 [512, 512], P('ctx'), may hold values from -6 to 6
- prompt_values: bfloat16 [512, 512], P('ctx'), may hold values from -6 to 6
- out_grad: bfloat16 [16, 2048, 2560], P('resp', 'ctx'), may hold values from -24 to 24
- lengths: int32 [16], P('resp'), may hold values from 256 to 2048, as said below
Outputs:
- attn_out: bfloat16 [16, 2048, 2560], P('resp', 'ctx')
- query_grad: bfloat16 [16, 2048, 2560], P('resp', 'ctx')
- resp_key_grad: bfloat16 [16, 2048, 512], P('resp', 'ctx')
- resp_value_grad: bfloat16 [16, 2048, 512], P('resp', 'ctx')
- prompt_key_grad: bfloat16 [512, 512], P('ctx')
- prompt_value_grad: bfloat16 [512, 512], P('ctx')
Inputs may be any that keep to these rules, and one draw needn't show every extreme that they name: `lengths`: some response has all 2048 tokens.
All inputs are finite; a program needn't handle non-finite values.
Results may differ from a plain program's by a relative error of at most 0.023.
Values may be sent and summed in bfloat16 or wider, within the bound.
A program may use at most 128 MiB of HBM per device.

v0:
```python
import math

import jax
import jax.numpy as jnp
from jax import lax
from jax.sharding import PartitionSpec as P

DH = 128
HQ = 20
HK = 4


NEG = -1e30


def score_block(query4, keys_blk, key_pos, row_pos, scale):
    keys3 = keys_blk.reshape(keys_blk.shape[0], query4.shape[1], query4.shape[3])
    raw = jnp.einsum("nkgd,mkd->kgnm", query4, keys3, preferred_element_type=jnp.float32) * scale
    allowed = key_pos[None, :] <= row_pos[:, None]
    return jnp.where(allowed[None, None], raw, jnp.float32(NEG))


def scan_blocks(keys_all, values_all, pos_all, step, init):
    total_rows = keys_all.shape[0]
    block = math.gcd(total_rows, 512)
    count = total_rows // block
    blocks = (
        keys_all.reshape(count, block, keys_all.shape[1]),
        values_all.reshape(count, block, values_all.shape[1]),
        pos_all.reshape(count, block),
    )
    return lax.scan(step, init, blocks)


def body(queries, resp_keys, resp_values, prompt_keys, prompt_values, out_grad, lengths):
    rows = queries.shape[1]
    group = HQ // HK
    width = HK * DH
    scale = DH ** (-0.5)
    cycle = lax.axis_size("ctx")
    first_row = lax.axis_index("ctx") * rows
    row_pos = first_row + jnp.arange(rows, dtype=jnp.int32)
    row_ok = row_pos < lengths[0]
    query4 = queries[0].reshape(rows, HK, group, DH)
    grad = jnp.where(row_ok[:, None], out_grad[0], jnp.zeros_like(out_grad[0]))
    grad4 = grad.reshape(rows, HK, group, DH)
    seq_rows = resp_keys.shape[1] * cycle
    prompt_rows = prompt_keys.shape[0] * cycle

    def stats_update(stats, keys_blk, key_pos):
        top, total = stats
        scores = score_block(query4, keys_blk, key_pos, row_pos, scale)
        new_top = jnp.maximum(top, jnp.max(scores, axis=-1))
        total = total * jnp.exp(top - new_top) + jnp.sum(
            jnp.exp(scores - new_top[..., None]), axis=-1
        )
        return (new_top, total)

    top0 = jnp.full((HK, group, rows), NEG, jnp.float32)
    total0 = jnp.zeros((HK, group, rows), jnp.float32)
    pieces = (
        lax.all_gather(prompt_keys, "ctx", axis=0, tiled=True),
        lax.all_gather(prompt_values, "ctx", axis=0, tiled=True),
    )
    top = top0
    total = total0
    key_pos = jnp.full((pieces[0].shape[0],), -1, jnp.int32)
    top, total = stats_update((top, total), pieces[0], key_pos)
    key_buf = pieces[0]
    value_buf = pieces[1]
    top, total, prompt_kbuf, prompt_vbuf = (top, total, key_buf, value_buf)
    pieces = (
        lax.all_gather(resp_keys[0], "ctx", axis=0, tiled=True),
        lax.all_gather(resp_values[0], "ctx", axis=0, tiled=True),
    )
    top, total, key_buf, value_buf = (
        top,
        total,
        jnp.zeros((seq_rows, width), jnp.bfloat16),
        jnp.zeros((seq_rows, width), jnp.bfloat16),
    )
    key_pos = jnp.arange(pieces[0].shape[0], dtype=jnp.int32)
    top, total = stats_update((top, total), pieces[0], key_pos)
    key_buf = pieces[0]
    value_buf = pieces[1]
    top, total, resp_kbuf, resp_vbuf = (top, total, key_buf, value_buf)
    lse = top + jnp.log(total)
    prompt_pos = jnp.full((prompt_rows,), -1, jnp.int32)
    resp_pos = jnp.arange(seq_rows, dtype=jnp.int32)

    def out_step(acc, blk):
        keys_blk, values_blk, key_pos = blk
        scores = score_block(query4, keys_blk, key_pos, row_pos, scale)
        prob = jnp.exp(scores - lse[..., None]).astype(jnp.bfloat16)
        values3 = values_blk.reshape(values_blk.shape[0], HK, DH)
        return (
            acc + jnp.einsum("kgnm,mkd->nkgd", prob, values3, preferred_element_type=jnp.float32),
            None,
        )

    mixed0 = jnp.zeros((rows, HK, group, DH), jnp.float32)
    mixed, unused = scan_blocks(prompt_kbuf, prompt_vbuf, prompt_pos, out_step, mixed0)
    mixed, unused = scan_blocks(resp_kbuf, resp_vbuf, resp_pos, out_step, mixed)
    attn_out = jnp.where(row_ok[:, None], mixed.reshape(rows, HQ * DH), jnp.float32(0.0)).astype(
        jnp.bfloat16
    )
    delta = jnp.einsum(
        "nkgd,nkgd->kgn",
        grad4,
        attn_out.reshape(rows, HK, group, DH),
        preferred_element_type=jnp.float32,
    )

    def grads_block(keys_blk, values_blk, key_pos):
        scores = score_block(query4, keys_blk, key_pos, row_pos, scale)
        prob = jnp.exp(scores - lse[..., None])
        prob_low = prob.astype(jnp.bfloat16)
        keys3 = keys_blk.reshape(keys_blk.shape[0], HK, DH)
        values3 = values_blk.reshape(values_blk.shape[0], HK, DH)
        dprob = jnp.einsum("nkgd,mkd->kgnm", grad4, values3, preferred_element_type=jnp.float32)
        dscore = (prob * (dprob - delta[..., None])).astype(jnp.bfloat16)
        dquery = (
            jnp.einsum("kgnm,mkd->nkgd", dscore, keys3, preferred_element_type=jnp.float32) * scale
        )
        dkey = (
            jnp.einsum("kgnm,nkgd->mkd", dscore, query4, preferred_element_type=jnp.float32) * scale
        )
        dvalue = jnp.einsum("kgnm,nkgd->mkd", prob_low, grad4, preferred_element_type=jnp.float32)
        both = jnp.concatenate(
            [dkey.reshape(keys_blk.shape[0], width), dvalue.reshape(keys_blk.shape[0], width)],
            axis=1,
        )
        return (dquery, both)

    def back_step(acc, blk):
        keys_blk, values_blk, key_pos = blk
        dquery, both = grads_block(keys_blk, values_blk, key_pos)
        return (acc + dquery, both)

    dquery0 = jnp.zeros((rows, HK, group, DH), jnp.float32)
    dquery, prompt_terms = scan_blocks(prompt_kbuf, prompt_vbuf, prompt_pos, back_step, dquery0)
    prompt_term = prompt_terms.reshape(prompt_rows, 2 * width)
    dquery, resp_terms = scan_blocks(resp_kbuf, resp_vbuf, resp_pos, back_step, dquery)
    resp_sum = lax.psum_scatter(
        resp_terms.reshape(seq_rows, 2 * width), "ctx", scatter_dimension=0, tiled=True
    )
    query_grad = dquery.reshape(rows, HQ * DH).astype(jnp.bfloat16)
    prompt_part = lax.psum_scatter(prompt_term, "ctx", scatter_dimension=0, tiled=True)
    prompt_sum = lax.psum(prompt_part, "resp")
    resp_key_grad = resp_sum[:, :width].astype(jnp.bfloat16)
    resp_value_grad = resp_sum[:, width:].astype(jnp.bfloat16)
    prompt_key_grad = prompt_sum[:, :width].astype(jnp.bfloat16)
    prompt_value_grad = prompt_sum[:, width:].astype(jnp.bfloat16)
    return (
        attn_out[None],
        query_grad[None],
        resp_key_grad[None],
        resp_value_grad[None],
        prompt_key_grad,
        prompt_value_grad,
    )


def solution(mesh):
    in_specs = (
        P("resp", "ctx", None),
        P("resp", "ctx", None),
        P("resp", "ctx", None),
        P("ctx", None),
        P("ctx", None),
        P("resp", "ctx", None),
        P("resp"),
    )
    out_specs = (
        P("resp", "ctx", None),
        P("resp", "ctx", None),
        P("resp", "ctx", None),
        P("resp", "ctx", None),
        P("ctx", None),
        P("ctx", None),
    )
    return jax.shard_map(body, mesh=mesh, in_specs=in_specs, out_specs=out_specs, check_vma=False)
```

profile of v0, /device:TPU:1, one launch (start us, length us, event | category | flops | bytes accessed | tf_op | source)
XLA Modules:
  0.0 321.2 jit_solution(5401829585454170042)
XLA Ops:
  11.4 24.9 %all_gather.12 = bf16[512,512]{1,0:T(8,128)(2,1)S(1)} all-gather(bf16[32,512]{1,0:T(8,128)(2,1)} %param.14), channel_id=1, replica_groups=mesh['resp'=16,'ctx'=16] {'ctx'}, dimensions={0}, use_global_device_ids=true | all-gather | bytes 557056 | tf_op jit(solution)/shard_map/all_gather | solution.py:62
  36.5 20.1 %all_gather.14 = bf16[512,512]{1,0:T(8,128)(2,1)S(1)} all-gather(bf16[32,512]{1,0:T(8,128)(2,1)} %param.15), channel_id=1, replica_groups=mesh['resp'=16,'ctx'=16] {'ctx'}, dimensions={0}, use_global_device_ids=true | all-gather | bytes 557056 | tf_op jit(solution)/shard_map/all_gather | solution.py:63
  59.7 3.2 bitcast_reduce_fusion
  62.9 4.8 %fusion.39 = (f32[4,5,128]{2,1,0:T(8,128)S(1)}, f32[4,2048,128,5]{2,1,3,0:T(8,128)S(1)}) fusion(pred[128,2048]{0,1:T(8,128)(4,1)S(1)} %iota_compare_fusion, bf16[2048,4,128,1]{0,2,3,1:T(8,128)(2,1)} %bitcast.261, bf16[128,4,5,128]{0,3,2,1:T(8,128)(2,1)S(1)} %bitcast.245), kind=kOutput, calls=%fused_computation.49 | convolution fusion | flops 1357903360 | bytes 23996416 | tf_op jit(solution)/shard_map/nkgd,mkd->kgnm/dot_general | solution.py:18
  67.7 3.7 %fusion.43 = f32[4,5,128]{2,1,0:T(8,128)S(1)} fusion(f32[4,512,128,5]{2,1,3,0:T(8,128)} %get-tuple-element.374, f32[4,5,128]{2,1,0:T(8,128)S(1)} %get-tuple-element.371, pred[128]{0:T(512)(128)(4,1)S(1)} %broadcast_compare_fusion.2), kind=kLoop, calls=%fused_computation.56 | loop fusion | flops 5240320 | bytes 5263488 | tf_op jit(solution)/shard_map/reduce_sum | solution.py:54
  71.4 4.5 %exponential_reduce_fusion = f32[4,5,128]{2,1,0:T(8,128)S(1)} fusion(f32[4,2048,128,5]{2,1,3,0:T(8,128)S(1)} %get-tuple-element.376, f32[4,5,128]{2,1,0:T(8,128)S(1)} %get-tuple-element.372, pred[128,2048]{0,1:T(8,128)(4,1)S(1)} %iota_compare_fusion), kind=kLoop, calls=%fused_computation.48 | loop fusion | flops 20968960 | bytes 21254144 | tf_op jit(solution)/shard_map/reduce_sum | solution.py:54
  80.9 4.5 %reshape.290 = bf16[4,512,512]{1,0,2:T(4,128)(2,1)} reshape(bf16[1,2048,512]{1,2,0:T(8,128)(2,1)} %all-gather.5.cloned.1.call-done) | data formatting | bytes 4194304 | tf_op jit(solution)/shard_map/reshape | solution.py:28
  85.4 3.3 %copy.171 = bf16[4,512,512]{1,2,0:T(8,128)(2,1)} copy(bf16[4,512,512]{1,0,2:T(4,128)(2,1)} %reshape.290) | data formatting | bytes 4194304
  88.7 6.5 %all-gather.7.cloned.1.call-done = bf16[1,2048,512]{2,1,0:T(8,128)(2,1)} async-done(((bf16[1,128,512]{2,1,0:T(8,128)(2,1)}), bf16[1,2048,512]{2,1,0:T(8,128)(2,1)}) %all-gather.7.cloned.1.call-update) | async-done | bytes 2097168 | tf_op jit(solution)/shard_map/all_gather | solution.py:74
  95.3 4.1 %copy.170 = bf16[4,512,512]{1,2,0:T(8,128)(2,1)} copy(bf16[4,512,512]{2,1,0:T(8,128)(2,1)} %bitcast.267) | data formatting | bytes 4194304
  99.4 21.0 %while.6 = (s32[]{:T(128)}, f32[128,4,5,128]{0,3,2,1:T(8,128)S(1)}, bf16[4,512,512]{1,2,0:T(8,128)(2,1)}, s32[4,512]{1,0:T(4,128)S(1)}, bf16[4,512,512]{1,2,0:T(...) while((s32[]{:T(128)}, ...), condition=%wide.region_5.6_spmd.clone, body=%wide.region_4.5_spmd.clone.sunk | while | flops 676724864 | bytes 6571113 | solution.py:32
  101.4 3.1 fusion.108
  106.7 3.1 fusion.108
  111.9 3.1 fusion.108
  117.1 3.1 fusion.108
  122.4 5.3 %fusion.50 = f32[4,128,512,1]{2,1,3,0:T(8,128)} fusion(bf16[128,4,5,128]{0,3,2,1:T(8,128)(2,1)S(1)} %get-tuple-element.536, f32[4,512,128,5]{2,1,3,0:T(8,128)} %get-tuple-element.374, f32[4,5,128]{2,1,0:T(8,128)} %get-tuple-element.581, pred[128]{0:T(512)(128)(4,1)S(1)} %broadcast_compare_fusion.3), kind=kOutput, calls=%fused_computation.75 | convolution fusion | flops 340787200 | bytes 6957184 | tf_op jit(solution)/shard_map/while/body/eval_jaxpr/kgnm,nkgd->mkd/dot_general | solution.py:128
  135.2 3.1 pad_maximum_fusion
  139.9 69.6 %while.7 = (s32[]{:T(128)}, f32[128,4,5,128]{0,3,2,1:T(8,128)}, f32[4,512,1024]{2,1,0:T(8,128)}, bf16[4,512,512]{1,2,0:T(8,128)(2,1)}, s32[4,512]{1,0:T(4,128)S(...) while((s32[]{:T(128)}, f32[128,4,5,128]{0,3,2,1:T(8,128)}, ...), condition=%wide.region_7.8_spmd.clone, body=%wide.region_6.7_spmd.clone.sunk | while | flops 1692336256 | bytes 52139704 | solution.py:32
  148.0 2.9 copy.245
  150.9 3.2 constant_dynamic-update-slice_fusion.2
  154.1 3.2 fusion.121
  165.4 2.9 copy.245
  168.3 3.2 constant_dynamic-update-slice_fusion.2
  171.5 3.2 fusion.121
  182.7 2.9 copy.245
  185.7 3.2 %constant_dynamic-update-slice_fusion.2 = f32[4,512,1024]{2,1,0:T(8,128)} fusion(f32[4,512,1024]{2,1,0:T(8,128)} %get-tuple-element.542, f32[1,512,1024]{2,1,0:T(8,128)} %copy.245, s32[]{:T(128)} %get-tuple-element.540), kind=kLoop, calls=%fused_computation.40.clone.1 | loop fusion | bytes 4194816 | tf_op jit(solution)/shard_map/while/body/jit(dynamic_update_index_in_dim)/dynamic_update_slice | solution.py:32
  188.9 3.2 fusion.121
  200.2 2.9 copy.245
  203.1 3.2 constant_dynamic-update-slice_fusion.2
  206.3 3.2 fusion.121
  213.2 73.2 %all-reduce.1 = bf16[32,1024]{1,0:T(8,128)(2,1)S(1)} all-reduce(f32[32,1024]{1,0:T(8,128)} %reduce-scatter.5.cloned.1.call-done), channel_id=1, replica_groups=mesh['resp'=16,'ctx'=16] {'resp'}, use_global_device_ids=true, to_apply=%region_10.11 | all-reduce | flops 32768 | bytes 196608 | tf_op jit(solution)/shard_map/psum | solution.py:149
  287.1 25.8 %reduce-scatter.3.cloned.1.call-done = f32[128,1024]{1,0:T(8,128)} async-done(((f32[2048,1024]{1,0:T(8,128)}), f32[128,1024]{1,0:T(8,128)}) %reduce-scatter.3.cloned.1.call-update) | async-done | bytes 524304 | tf_op jit(solution)/shard_map/reduce_scatter | solution.py:144
  (143 shorter events, 69.1 us)
Async XLA Ops:
  7.2 51.4 %copy-start.4 = (bf16[1,128,2560]{2,1,0:T(8,128)(2,1)S(1)}, bf16[1,128,2560]{2,1,0:T(8,128)(2,1)}, u32[]{:S(2)}) copy-start(bf16[1,128,2560]{2,1,0:T(8,128)(2,1)} %param.16) | copy-start | bytes 1966084
  7.2 55.7 %all-gather.5.cloned.1.call-start = ((), (), s32[]{:S(2)}) async-start(), calls=%async_computation.4 | async-start | bytes 2228224 | tf_op jit(solution)/shard_map/all_gather | solution.py:73
  9.0 86.3 %all-gather.7.cloned.1.call-start = ((), (), s32[]{:S(2)}) async-start(), calls=%async_computation.5 | async-start | bytes 2228224 | tf_op jit(solution)/shard_map/all_gather | solution.py:74
  9.7 203.5 %reduce-scatter.5.cloned.1.call-start = ((), (), s32[]{:S(2)}) async-start(), calls=%async_computation.3 | async-start | bytes 2228224 | tf_op jit(solution)/shard_map/reduce_scatter | solution.py:148
  56.9 19.1 %copy-start.7 = (bf16[512,512]{0,1:T(8,128)(2,1)}, bf16[512,512]{0,1:T(8,128)(2,1)S(1)}, u32[]{:S(2)}) copy-start(bf16[512,512]{0,1:T(8,128)(2,1)S(1)} %copy.166) | copy-start | bytes 1572868
  67.7 8.9 %slice-start = ((s8[5242880]{0:T(1024)(128)(4,1)}), s8[4194304]{0:T(1024)(128)(4,1)S(1)}, s32[]{:S(2)}) async-start(s8[5242880]{0:T(1024)(128)(4,1)} %bitcast.252), calls=%async_computation.6 | async-start | bytes 8388608
  71.4 5.2 %slice-start.1 = ((s8[5242880]{0:T(1024)(128)(4,1)}), s8[1048576]{0:T(1024)(128)(4,1)S(1)}, s32[]{:S(2)}) async-start(s8[5242880]{0:T(1024)(128)(4,1)} %bitcast.252), calls=%async_computation.7 | async-start | bytes 2097152
  76.0 0.6 copy-start.11
  120.4 7.2 %copy-start.2 = (f32[128,4,5,128]{0,3,2,1:T(8,128)}, f32[128,4,5,128]{0,3,2,1:T(8,128)S(1)}, u32[]{:S(2)}) copy-start(f32[128,4,5,128]{0,3,2,1:T(8,128)S(1)} %get-tuple-element.157) | copy-start | bytes 3932164
  120.4 7.2 %slice-start.2 = ((s8[5242880]{0:T(1024)(128)(4,1)}), s8[4194304]{0:T(1024)(128)(4,1)S(1)}, s32[]{:S(2)}) async-start(s8[5242880]{0:T(1024)(128)(4,1)} %bitcast.254), calls=%async_computation.8 | async-start | bytes 8388608
  120.4 7.2 %copy-start.8 = (bf16[512,512]{0,1:T(8,128)(2,1)S(1)}, bf16[512,512]{0,1:T(8,128)(2,1)}, u32[]{:S(2)}) copy-start(bf16[512,512]{0,1:T(8,128)(2,1)} %copy-done.7) | copy-start | bytes 1572868
  120.5 7.2 %copy-start.12 = (f32[4,5,128]{2,1,0:T(8,128)S(1)}, f32[4,5,128]{2,1,0:T(8,128)}, u32[]{:S(2)}) copy-start(f32[4,5,128]{2,1,0:T(8,128)} %get-tuple-element.581) | copy-start | bytes 30724
  122.3 7.0 %copy-start.5 = (bf16[128,4,5,128]{0,3,2,1:T(8,128)(2,1)}, bf16[128,4,5,128]{0,3,2,1:T(8,128)(2,1)S(1)}, u32[]{:S(2)}) copy-start(bf16[128,4,5,128]{0,3,2,1:T(8,128)(2,1)S(1)} %get-tuple-element.536) | copy-start | bytes 1966084
  122.4 7.0 %copy-start.9 = (f32[4,5,128]{2,1,0:T(8,128)}, f32[4,5,128]{2,1,0:T(8,128)S(1)}, u32[]{:S(2)}) copy-start(f32[4,5,128]{2,1,0:T(8,128)S(1)} %get-tuple-element.537) | copy-start | bytes 30724
  122.4 5.3 %slice-start.3 = ((s8[5242880]{0:T(1024)(128)(4,1)}), s8[1048576]{0:T(1024)(128)(4,1)S(1)}, s32[]{:S(2)}) async-start(s8[5242880]{0:T(1024)(128)(4,1)} %bitcast.254), calls=%async_computation.9 | async-start | bytes 2097152
  133.9 5.9 %copy-start.10 = (f32[4,5,128]{2,1,0:T(8,128)S(1)}, f32[4,5,128]{2,1,0:T(8,128)}, u32[]{:S(2)}) copy-start(f32[4,5,128]{2,1,0:T(8,128)} %copy-done.9) | copy-start | bytes 30724
  133.9 5.9 %copy-start.13 = (f32[4,5,128]{2,1,0:T(8,128)S(1)}, f32[4,5,128]{2,1,0:T(8,128)}, u32[]{:S(2)}) copy-start(f32[4,5,128]{2,1,0:T(8,128)} %get-tuple-element.581) | copy-start | bytes 30724
  138.3 174.5 %reduce-scatter.3.cloned.1.call-start = ((), (), s32[]{:S(2)}) async-start(), calls=%async_computation.2 | async-start | bytes 8912896 | tf_op jit(solution)/shard_map/reduce_scatter | solution.py:144
  139.9 2.4 copy-start.6
  141.2 1.1 copy-start
  157.3 2.4 copy-start.6
  158.6 1.1 copy-start
  174.7 2.4 copy-start.6
  176.0 1.1 copy-start
  192.1 2.4 copy-start.6
  193.4 1.1 copy-start
  209.5 1.3 copy-start.1
  209.5 2.5 copy-start.3
Sparse Core Ops, SparseCore 0:
  10.4 45.1 all-gather.4
  57.4 37.8 all-gather.6
  138.5 63.2 reduce-scatter.4
  209.6 103.1 reduce-scatter.2
where the time goes:
time: 323 us; the launch traced here: 321 us
  blocking collectives  118 us (37%)
  local copies, waits for them, and re-layouts  65.2 us (20%)
  matrix products  64.7 us (20%)
  waiting for transfers between devices  33.1 us (10%)
  other arithmetic  24.4 us (8%)
  between operations  14.7 us (5%)
    psum x1, blocking collectives, body(): prompt_sum = lax.psum(prompt_part, 'resp')  73.2 us
    reduce_scatter x1, waiting for transfers between devices, body(): lax.psum_scatter(resp_terms.reshape(seq_rows, 2 * width), 'ctx', scatter_...  25.8 us
    all_gather x1, blocking collectives, body(): lax.all_gather(prompt_keys, 'ctx', axis=0, tiled=True)  24.9 us
    dynamic_update_slice x8, local copies, waits for them, and re-layouts, scan_blocks(): return lax.scan(step, init, blocks)  24.5 us
    all_gather x1, blocking collectives, body(): lax.all_gather(prompt_values, 'ctx', axis=0, tiled=True)  20.1 us
    unnamed x42, local copies, waits for them, and re-layouts  20.1 us
    dot_general x5, matrix products, out_step(): jnp.einsum('kgnm,mkd->nkgd', prob, values3, preferred_element_type=jnp.fl...  15.1 us
    dot_general x5, matrix products, grads_block(): jnp.einsum('kgnm,mkd->nkgd', dscore, keys3, preferred_element_type=jnp.fl...  13.8 us
  transfers between devices with their start and end apart: 4, of which 2 were waited for; matrix products, arithmetic and copies ran while one was open for 33% of the time, Pallas kernels for 0%

commit v1 on v0

v1 whole, which is shorter than its diff:
```python
import functools
import math

import jax
import jax.numpy as jnp
from jax import lax
from jax.experimental import pallas as pl
from jax.experimental.pallas import tpu as pltpu
from jax.sharding import PartitionSpec as P

DH = 128
HQ = 20
HK = 4
G = HQ // HK
GW = G * DH
R = 128
M = G * R
CH = 512
NC = 5
PR = 32
BF = jnp.bfloat16
F32 = jnp.float32
MESH = pl.DeviceIdType.MESH
SCALE = DH**-0.5
CEXP = SCALE * math.log2(math.e)
NEG = -1e30
NT = (((1,), (1,)), ((), ()))
NN = (((1,), (0,)), ((), ()))


def dot(a, b, dims):
    return lax.dot_general(a, b, dims, preferred_element_type=F32)


def rows_of(i, size):
    return pl.ds(pl.multiple_of(i * size, size), size)


def attend_block(b, j, length, qin, gin, kbuf, ob, dqb, qs, gs, s_scr, p_scr, dkt, dvt):
    for h in range(G):
        qs[h * R : (h + 1) * R, :] = qin[b, :, h * DH : (h + 1) * DH]
    q = qs[...]

    def scores(k, m):
        s = dot(q, kbuf[0, k], NT)
        s_scr[k] = s
        for t in range(CH // 128):
            m = jnp.maximum(m, s[:, t * 128 : (t + 1) * 128])
        return m

    m = lax.fori_loop(0, b + 1, scores, jnp.full((M, 128), NEG, F32))
    last = b + 1
    s = dot(q, kbuf[0, last], NT)
    row = lax.broadcasted_iota(jnp.int32, (R, CH), 0) + j * R
    col = lax.broadcasted_iota(jnp.int32, (R, CH), 1)
    s = jnp.where(jnp.concatenate([col <= row] * G, axis=0), s, NEG)
    s_scr[last] = s
    for t in range(CH // 128):
        m = jnp.maximum(m, s[:, t * 128 : (t + 1) * 128])
    top = jnp.max(m, axis=1, keepdims=True) * CEXP

    def mix(k, carry):
        o, l = carry
        p = jnp.exp2(s_scr[k] * CEXP - top)
        for t in range(CH // 128):
            l = l + p[:, t * 128 : (t + 1) * 128]
        p = p.astype(BF)
        p_scr[k] = p
        return o + dot(p, kbuf[1, k], NN), l

    o, l = lax.fori_loop(0, b + 2, mix, (jnp.zeros((M, DH), F32), jnp.zeros((M, 128), F32)))
    rl = 1.0 / jnp.sum(l, axis=1, keepdims=True)
    token = lax.broadcasted_iota(jnp.int32, (R, 1), 0) + (4 * b + j) * R
    valid = jnp.concatenate([token < length] * G, axis=0)
    o = jnp.where(valid, o * rl, 0.0).astype(BF)
    for h in range(G):
        ob[b, :, h * DH : (h + 1) * DH] = o[h * R : (h + 1) * R, :]
        gs[h * R : (h + 1) * R, :] = gin[b, :, h * DH : (h + 1) * DH]
    gl = jnp.where(valid, gs[...].astype(F32) * rl, 0.0).astype(BF)
    delta = jnp.sum(gl.astype(F32) * o.astype(F32), axis=1, keepdims=True)
    qt = q.astype(F32).T.astype(BF)
    gt = gl.astype(F32).T.astype(BF)

    def grads(k, dq):
        kc = kbuf[0, k]
        p = p_scr[k]
        dp = dot(gl, kbuf[1, k], NT)
        ds = (p.astype(F32) * (dp - delta)).astype(BF)
        dvt[k] += dot(gt, p, NN)
        dkt[k] += dot(qt, ds, NN)
        return dq + dot(ds, kc, NN)

    dq = lax.fori_loop(0, b + 2, grads, jnp.zeros((M, DH), F32))
    dq = (dq * SCALE).astype(BF)
    for h in range(G):
        dqb[b, :, h * DH : (h + 1) * DH] = dq[h * R : (h + 1) * R, :]


def kernel(
    n,
    len_ref, q_ref, rk_ref, rv_ref, pk_ref, pv_ref, g_ref,
    out_ref, dq_ref, drk_ref, drv_ref, dpk_ref, dpv_ref,
    qin, gin, kbuf, ob, dqb, qs, gs, s_scr, p_scr, dkt, dvt,
    s1, r1, s2, r2, s3, ps, pin, pown, pall,
    loc, kv_send, kv_recv, qg_send, qg_recv, f_send, f_recv, o_send, o_recv,
    c_send, c_recv, x_send, x_recv, rs_send, rs_recv, ag_send, ag_recv, px_send, px_recv,
    fin,
):
    c = lax.axis_index("ctx")
    r = lax.axis_index("resp")
    x, j = c // 4, c % 4
    zl, core = j // 2, j % 2
    core_mate = x * 4 + zl * 2 + (1 - core)
    z_mate = x * 4 + (1 - zl) * 2 + core
    j_c = zl * 2 + (1 - core)
    j_z = (1 - zl) * 2 + core
    ORDER = (1, 3, 2)
    prow = 256 // n

    def other(d):
        return (x + d) % 4

    def source(d):
        return (x + 4 - d) % 4

    def send(src, dst, ssem, rsem, **where):
        return pltpu.make_async_remote_copy(
            src_ref=src, dst_ref=dst, send_sem=ssem, recv_sem=rsem,
            device_id=where, device_id_type=MESH,
        )

    barrier = pltpu.get_barrier_semaphore()
    for d in ORDER:
        pl.semaphore_signal(barrier, inc=1, device_id={"ctx": other(d) * 4 + j}, device_id_type=MESH)
    for mate in (core_mate, z_mate):
        pl.semaphore_signal(barrier, inc=1, device_id={"ctx": mate}, device_id_type=MESH)
    for e in range(1, n):
        pl.semaphore_signal(barrier, inc=1, device_id={"resp": (r + e) % n}, device_id_type=MESH)
    pl.semaphore_wait(barrier, 5 + n - 1)

    def head_cols(h):
        return rows_of(h, DH)

    def kv_pairs(h, at):
        cols = head_cols(h)
        rows = rows_of(j, R)
        prows = pl.ds(pl.multiple_of(j * R + at * PR, PR), PR)
        return (
            (rk_ref.at[0, :, cols], kbuf.at[0, 1 + at, rows, :]),
            (rv_ref.at[0, :, cols], kbuf.at[1, 1 + at, rows, :]),
            (pk_ref.at[:, cols], kbuf.at[0, 0, prows, :]),
            (pv_ref.at[:, cols], kbuf.at[1, 0, prows, :]),
        )

    kv_copies = {}
    for d in ORDER:
        kv_copies[d] = [
            send(src, dst, kv_send.at[d - 1, i], kv_recv.at[d - 1, i], ctx=other(d) * 4 + j)
            for i, (src, dst) in enumerate(kv_pairs(other(d), x))
        ]
        for cp in kv_copies[d]:
            cp.start()
    own = [pltpu.make_async_copy(src, dst, loc.at[i]) for i, (src, dst) in enumerate(kv_pairs(x, x))]
    for cp in own:
        cp.start()

    def qg_pairs(h, at):
        cols = rows_of(h, GW)
        return ((q_ref.at[0, :, cols], qin.at[at]), (g_ref.at[0, :, cols], gin.at[at]))

    qg_copies = []
    for d in ORDER:
        for i, (src, dst) in enumerate(qg_pairs(other(d), x)):
            cp = send(src, dst, qg_send.at[d, i], qg_recv.at[d, i], ctx=other(d) * 4 + j)
            cp.start()
            qg_copies.append(cp)
    for i, (src, dst) in enumerate(qg_pairs(x, x)):
        pltpu.make_async_copy(src, dst, qg_recv.at[0, i]).start()

    fwd = []

    def hand_on(slot, chunk, rows_j, kind, mate):
        view = kbuf.at[:, chunk, rows_of(rows_j, R), :]
        cp = send(view, view, f_send.at[slot, kind], f_recv.at[slot, kind], ctx=mate)
        cp.start()
        fwd.append(cp)

    def wait_handed(slot, chunk, rows_j, kind, mate):
        view = kbuf.at[:, chunk, rows_of(rows_j, R), :]
        send(view, view, f_send.at[slot, kind], f_recv.at[slot, kind], ctx=mate).wait_recv()

    for cp in own:
        cp.wait()
    hand_on(0, 1 + x, j, 0, core_mate)
    hand_on(0, 1 + x, j, 1, z_mate)
    for d in ORDER:
        for i, (src, dst) in enumerate(kv_pairs(x, source(d))):
            send(src, dst, kv_send.at[d - 1, i], kv_recv.at[d - 1, i], ctx=c).wait_recv()
        hand_on(d, 1 + source(d), j, 0, core_mate)
        hand_on(d, 1 + source(d), j, 1, z_mate)
    hand_on(4, 0, j, 0, core_mate)
    hand_on(4, 0, j, 1, z_mate)
    slots = [(0, 1 + x)] + [(d, 1 + source(d)) for d in ORDER] + [(4, 0)]
    for slot, chunk in slots:
        wait_handed(slot, chunk, j_z, 1, z_mate)
        hand_on(slot, chunk, j_z, 2, core_mate)
    for slot, chunk in slots:
        wait_handed(slot, chunk, j_c, 0, core_mate)
        wait_handed(slot, chunk, 3 - j, 2, core_mate)

    dkt[...] = jnp.zeros_like(dkt)
    dvt[...] = jnp.zeros_like(dvt)
    length = len_ref[0]

    def result_pairs(b, h):
        cols = rows_of(h, GW)
        return ((ob.at[b], out_ref.at[0, :, cols]), (dqb.at[b], dq_ref.at[0, :, cols]))

    def step(i, carry):
        d = jnp.where(i == 0, 1, jnp.where(i == 1, 3, jnp.where(i == 2, 2, 0)))
        b = (x + 4 - d) % 4
        for t, (src, dst) in enumerate(qg_pairs(x, b)):
            pltpu.make_async_copy(src, dst, qg_recv.at[d, t]).wait()
        attend_block(b, j, length, qin, gin, kbuf, ob, dqb, qs, gs, s_scr, p_scr, dkt, dvt)

        @pl.when(i < 3)
        def _():
            for t, (src, dst) in enumerate(result_pairs(b, x)):
                send(src, dst, o_send.at[d, t], o_recv.at[d, t], ctx=b * 4 + j).start()

        return carry

    lax.fori_loop(0, 4, step, 0)
    finals = []
    for t, (src, dst) in enumerate(result_pairs(x, x)):
        cp = pltpu.make_async_copy(src, dst, fin.at[t])
        cp.start()
        finals.append(cp)

    def part(k, kv, jj):
        lanes = rows_of(jj, R)
        if kv == 0:
            return dkt[k, :, lanes].T * SCALE
        return dvt[k, :, lanes].T

    for k in range(NC):
        for kv in range(2):
            for zz in range(2):
                s1[zz, kv, k] = part(k, kv, 2 * zz + 1 - core).astype(BF)
    cp1 = send(s1, r1, c_send.at[0], c_recv.at[0], ctx=core_mate)
    cp1.start()
    cp1.wait_recv()
    for k in range(NC):
        for kv in range(2):
            s2[kv, k] = (part(k, kv, j_z) + r1[1 - zl, kv, k].astype(F32)).astype(BF)
    cp2 = send(s2, r2, c_send.at[1], c_recv.at[1], ctx=z_mate)
    cp2.start()
    cp2.wait_recv()

    def total(k, kv):
        return part(k, kv, j) + r1[zl, kv, k].astype(F32) + r2[kv, k].astype(F32)

    for kv in range(2):
        t = total(0, kv)
        pown[kv * R : (kv + 1) * R, :] = t
        ps[kv * R : (kv + 1) * R, :] = t.astype(BF)

    def scatter(e, carry):
        to = (r + e) % n
        send(ps.at[rows_of(to, prow), :], pin.at[e], rs_send.at[e], rs_recv.at[e], resp=to).start()
        return carry

    lax.fori_loop(1, n, scatter, 0)

    for k in range(1, NC):
        for kv in range(2):
            s3[k - 1, kv] = total(k, kv).astype(BF)

    def row_pairs(at, h):
        cols = head_cols(h)
        return ((s3.at[at, 0], drk_ref.at[0, :, cols]), (s3.at[at, 1], drv_ref.at[0, :, cols]))

    xs_copies = []
    for d in ORDER:
        for t, (src, dst) in enumerate(row_pairs(other(d), x)):
            cp = send(src, dst, x_send.at[d, t], x_recv.at[d, t], ctx=other(d) * 4 + j)
            cp.start()
            xs_copies.append(cp)
    for t, (src, dst) in enumerate(row_pairs(x, x)):
        cp = pltpu.make_async_copy(src, dst, fin.at[2 + t])
        cp.start()
        finals.append(cp)

    def gather_sum(e, acc):
        send(ps.at[rows_of(r, prow), :], pin.at[e], rs_send.at[e], rs_recv.at[e], resp=r).wait_recv()
        return acc + pin[e].astype(F32)

    psum = lax.fori_loop(1, n, gather_sum, pown[rows_of(r, prow), :])
    pall[rows_of(r, prow), :] = psum.astype(BF)

    def spread(e, carry):
        to = (r + e) % n
        view = pall.at[rows_of(r, prow), :]
        send(view, view, ag_send.at[e], ag_recv.at[e], resp=to).start()
        return carry

    lax.fori_loop(1, n, spread, 0)

    def collect(e, carry):
        view = pall.at[rows_of((r + n - e) % n, prow), :]
        send(view, view, ag_send.at[e], ag_recv.at[e], resp=r).wait_recv()
        return carry

    lax.fori_loop(1, n, collect, 0)

    def prompt_pairs(at, h):
        cols = head_cols(h)
        return (
            (pall.at[rows_of(at, PR), :], dpk_ref.at[:, cols]),
            (pall.at[rows_of(4 + at, PR), :], dpv_ref.at[:, cols]),
        )

    for d in ORDER:
        for t, (src, dst) in enumerate(prompt_pairs(other(d), x)):
            cp = send(src, dst, px_send.at[d, t], px_recv.at[d, t], ctx=other(d) * 4 + j)
            cp.start()
            xs_copies.append(cp)
    for t, (src, dst) in enumerate(prompt_pairs(x, x)):
        cp = pltpu.make_async_copy(src, dst, fin.at[4 + t])
        cp.start()
        finals.append(cp)

    for d in ORDER:
        for t in range(2):
            src, dst = result_pairs(source(d), other(d))[t]
            cp = send(src, dst, o_send.at[d, t], o_recv.at[d, t], ctx=source(d) * 4 + j)
            cp.wait_recv()
            cp.wait_send()
            src, dst = row_pairs(x, source(d))[t]
            send(src, dst, x_send.at[d, t], x_recv.at[d, t], ctx=c).wait_recv()
            src, dst = prompt_pairs(x, source(d))[t]
            send(src, dst, px_send.at[d, t], px_recv.at[d, t], ctx=c).wait_recv()
    for cp in finals:
        cp.wait()
    for d in ORDER:
        for cp in kv_copies[d]:
            cp.wait_send()
    for cp in qg_copies + fwd + [cp1, cp2] + xs_copies:
        cp.wait_send()

    def sent(e, carry):
        send(ps.at[rows_of(r, prow), :], pin.at[e], rs_send.at[e], rs_recv.at[e], resp=r).wait_send()
        view = pall.at[rows_of(r, prow), :]
        send(view, view, ag_send.at[e], ag_recv.at[e], resp=r).wait_send()
        return carry

    lax.fori_loop(1, n, sent, 0)


def body(n, queries, resp_keys, resp_values, prompt_keys, prompt_values, out_grad, lengths):
    shape = jax.ShapeDtypeStruct
    anywhere = pl.BlockSpec(memory_space=pl.ANY)
    vmem = pltpu.VMEM
    dma = pltpu.SemaphoreType.DMA
    return pl.pallas_call(
        functools.partial(kernel, n),
        out_shape=(
            shape((1, R, HQ * DH), BF),
            shape((1, R, HQ * DH), BF),
            shape((1, R, HK * DH), BF),
            shape((1, R, HK * DH), BF),
            shape((PR, HK * DH), BF),
            shape((PR, HK * DH), BF),
        ),
        in_specs=[pl.BlockSpec(memory_space=pltpu.SMEM)] + [anywhere] * 6,
        out_specs=(anywhere,) * 6,
        scratch_shapes=[
            vmem((4, R, GW), BF), vmem((4, R, GW), BF), vmem((2, NC, CH, DH), BF),
            vmem((4, R, GW), BF), vmem((4, R, GW), BF), vmem((M, DH), BF), vmem((M, DH), BF),
            vmem((NC, M, CH), F32), vmem((NC, M, CH), BF), vmem((NC, DH, CH), F32), vmem((NC, DH, CH), F32),
            vmem((2, 2, NC, R, DH), BF), vmem((2, 2, NC, R, DH), BF),
            vmem((2, NC, R, DH), BF), vmem((2, NC, R, DH), BF), vmem((4, 2, R, DH), BF),
            vmem((2 * R, DH), BF), vmem((n, 256 // n, DH), BF), vmem((2 * R, DH), F32), vmem((2 * R, DH), BF),
            dma((4,)), dma((3, 4)), dma((3, 4)), dma((4, 2)), dma((4, 2)), dma((5, 3)), dma((5, 3)),
            dma((4, 2)), dma((4, 2)), dma((2,)), dma((2,)), dma((4, 2)), dma((4, 2)),
            dma((n,)), dma((n,)), dma((n,)), dma((n,)), dma((4, 2)), dma((4, 2)), dma((6,)),
        ],
        compiler_params=pltpu.CompilerParams(
            collective_id=0, has_side_effects=True, vmem_limit_bytes=56 << 20
        ),
    )(lengths, queries, resp_keys, resp_values, prompt_keys, prompt_values, out_grad)


def solution(mesh):
    seq = P("resp", "ctx", None)
    return jax.shard_map(
        functools.partial(body, mesh.shape["resp"]),
        mesh=mesh,
        in_specs=(seq, seq, seq, P("ctx", None), P("ctx", None), seq, P("resp")),
        out_specs=(seq, seq, seq, seq, P("ctx", None), P("ctx", None)),
        check_vma=False,
    )
```

time: 323 us -> 86.4 us (0.27)
  blocking collectives: 118 us -> 0 us
  Pallas kernels: 0 us -> 77.4 us
  matrix products: 64.7 us -> 0 us
  local copies, waits for them, and re-layouts: 65.2 us -> 6.15 us
  waiting for transfers between devices: 33.1 us -> 0 us
  other arithmetic: 24.4 us -> 0 us
  between operations: 14.7 us -> 1.3 us
    pallas_call x0 -> x1, Pallas kernels: none -> 77.4 us  [body(): pl.pallas_call(functools.partial(kernel, n), out_shape=(shape((1, R, HQ *...]
    psum x1 -> x0, blocking collectives: 73.2 us -> none  [body(): prompt_sum = lax.psum(prompt_part, 'resp')]
    dot_general x31 -> x0, matrix products: 64.7 us -> none  [the longest x5 15.1 us: out_step(): jnp.einsum('kgnm,mkd->nkgd', prob, values3, preferred_element_type=jnp.fl...]
    all_gather x2 -> x0, blocking collectives: 45 us -> none  [the longest x1 24.9 us: body(): lax.all_gather(prompt_keys, 'ctx', axis=0, tiled=True)]
    reduce_scatter x2 -> x0, waiting for transfers between devices: 25.8 us -> none  [the longest x1 25.8 us: body(): lax.psum_scatter(resp_terms.reshape(seq_rows, 2 * width), 'ctx', scatter_...]
    dynamic_update_slice x8 -> x0, local copies, waits for them, and re-layouts: 24.5 us -> none  [scan_blocks(): return lax.scan(step, init, blocks)]
    unnamed x42 -> x16, local copies, waits for them, and re-layouts: 20.1 us -> 6.15 us
    dynamic_slice x16 -> x0, local copies, waits for them, and re-layouts: 10.5 us -> none  [scan_blocks(): return lax.scan(step, init, blocks)]
  transfers between devices with their start and end apart: 4 -> 0, of which waited for: 2 -> 0; matrix products, arithmetic and copies ran while one was open for 33% -> 0% of each run, Pallas kernels for 0% -> 0%
where the time goes in v1:
time: 86.4 us; the launch traced here: 84.9 us
  Pallas kernels  77.4 us (90%)
  local copies, waits for them, and re-layouts  6.15 us (7%)
  between operations  1.3 us (2%)
    pallas_call x1, Pallas kernels, body(): pl.pallas_call(functools.partial(kernel, n), out_shape=(shape((1, R, HQ *...  77.4 us
    unnamed x16, local copies, waits for them, and re-layouts  6.15 us

profile of v1, /device:TPU:1, one launch (start us, length us, event | category | flops | bytes accessed | tf_op | source)
XLA Modules:
  0.0 84.9 jit_solution(6318316345264111085)
XLA Ops:
  1.3 77.4 %shard_map.118 = (bf16[1,128,2560]{2,1,0:T(8,128)(2,1)}, bf16[1,128,2560]{2,1,0:T(8,128)(2,1)}, bf16[1,128,512]{2,1,0:T(8,128)(2,1)}, bf16[1,128,512]{2,1,0:T(8,...) custom-call(s32[1]{0:T(128)S(6)} %copy.19.len_ref, bf16[1,128,2560]{2,1,0:T(8,128)(2,1)} %q_ref.1, ...), custom_call_target="tpu_custom_call" | custom-call | tf_op jit(solution)/shard_map/pallas_call | solution.py:365
  78.7 0.0 copy-start
  78.7 2.0 %copy.20 = bf16[1,128,2560]{2,1,0:T(8,128)(2,1)} copy(bf16[1,128,2560]{2,1,0:T(8,128)(2,1)} %get-tuple-element.12) | data formatting | bytes 1310720
  80.8 0.0 copy-done
  80.8 0.0 copy-start.2
  80.8 0.8 copy.21
  81.6 0.2 copy-done.2
  81.8 0.0 copy-start.1
  81.8 0.7 copy.22
  82.5 0.3 copy-done.1
  82.7 0.0 copy-start.4
  82.7 0.7 copy.23
  83.4 0.1 copy-done.4
  83.5 0.0 copy-start.3
  83.5 0.6 copy.24
  84.1 0.2 copy-done.3
  84.3 0.6 copy.25
Async XLA Ops:
  78.7 2.0 %copy-start = (bf16[1,128,2560]{2,1,0:T(8,128)(2,1)S(1)}, bf16[1,128,2560]{2,1,0:T(8,128)(2,1)}, u32[]{:S(2)}) copy-start(bf16[1,128,2560]{2,1,0:T(8,128)(2,1)} %get-tuple-element.13) | copy-start | bytes 1966084
  80.8 1.0 %copy-start.2 = (bf16[1,128,512]{2,1,0:T(8,128)(2,1)S(1)}, bf16[1,128,512]{2,1,0:T(8,128)(2,1)}, u32[]{:S(2)}) copy-start(bf16[1,128,512]{2,1,0:T(8,128)(2,1)} %get-tuple-element.14) | copy-start | bytes 393220
  81.8 1.0 %copy-start.1 = (bf16[1,128,512]{2,1,0:T(8,128)(2,1)S(1)}, bf16[1,128,512]{2,1,0:T(8,128)(2,1)}, u32[]{:S(2)}) copy-start(bf16[1,128,512]{2,1,0:T(8,128)(2,1)} %get-tuple-element.15) | copy-start | bytes 393220
  82.7 0.8 copy-start.4
  83.5 0.8 copy-start.3

commit v2 on v1

--- a/solution.py
+++ b/solution.py
@@ -26,6 +26,7 @@
 NEG = -1e30
 NT = (((1,), (1,)), ((), ()))
 NN = (((1,), (0,)), ((), ()))
+TN = (((0,), (0,)), ((), ()))
 
 
 def dot(a, b, dims):
@@ -36,10 +37,16 @@
     return pl.ds(pl.multiple_of(i * size, size), size)
 
 
-def attend_block(b, j, length, qin, gin, kbuf, ob, dqb, qs, gs, s_scr, p_scr, dkt, dvt):
+def attend_block(b, j, length, qin, gin, kbuf, ob, qs, gs, de, s_scr, p_scr):
+    base = b * M
+    mine = rows_of(b, M)
+
+    def head(h):
+        return pl.ds(pl.multiple_of(base + h * R, R), R)
+
     for h in range(G):
-        qs[h * R : (h + 1) * R, :] = qin[b, :, h * DH : (h + 1) * DH]
-    q = qs[...]
+        qs[head(h), :] = qin[b, :, h * DH : (h + 1) * DH]
+    q = qs[mine, :]
 
     def scores(k, m):
         s = dot(q, kbuf[0, k], NT)
@@ -65,7 +72,7 @@
         for t in range(CH // 128):
             l = l + p[:, t * 128 : (t + 1) * 128]
         p = p.astype(BF)
-        p_scr[k] = p
+        p_scr[k, mine, :] = p
         return o + dot(p, kbuf[1, k], NN), l
 
     o, l = lax.fori_loop(0, b + 2, mix, (jnp.zeros((M, DH), F32), jnp.zeros((M, 128), F32)))
@@ -75,33 +82,38 @@
     o = jnp.where(valid, o * rl, 0.0).astype(BF)
     for h in range(G):
         ob[b, :, h * DH : (h + 1) * DH] = o[h * R : (h + 1) * R, :]
-        gs[h * R : (h + 1) * R, :] = gin[b, :, h * DH : (h + 1) * DH]
-    gl = jnp.where(valid, gs[...].astype(F32) * rl, 0.0).astype(BF)
+        gs[head(h), :] = gin[b, :, h * DH : (h + 1) * DH]
+    gl = jnp.where(valid, gs[mine, :].astype(F32) * rl, 0.0).astype(BF)
+    gs[mine, :] = gl
     delta = jnp.sum(gl.astype(F32) * o.astype(F32), axis=1, keepdims=True)
-    qt = q.astype(F32).T.astype(BF)
-    gt = gl.astype(F32).T.astype(BF)
-
-    def grads(k, dq):
-        kc = kbuf[0, k]
-        p = p_scr[k]
-        dp = dot(gl, kbuf[1, k], NT)
-        ds = (p.astype(F32) * (dp - delta)).astype(BF)
-        dvt[k] += dot(gt, p, NN)
-        dkt[k] += dot(qt, ds, NN)
-        return dq + dot(ds, kc, NN)
-
-    dq = lax.fori_loop(0, b + 2, grads, jnp.zeros((M, DH), F32))
-    dq = (dq * SCALE).astype(BF)
-    for h in range(G):
-        dqb[b, :, h * DH : (h + 1) * DH] = dq[h * R : (h + 1) * R, :]
+    de[mine, :] = jnp.broadcast_to(delta, (M, 128))
+
+
+def grad_terms(k, rows, kbuf, qs, gs, de, p_scr, dka, dva, fresh):
+    gl = gs[rows, :]
+    delta = de[rows, :]
+    p = p_scr[k, rows, :]
+    dp = dot(gl, kbuf[1, k], NT)
+    ds = jnp.concatenate(
+        [
+            (p[:, t : t + 128].astype(F32) * (dp[:, t : t + 128] - delta)).astype(BF)
+            for t in range(0, CH, 128)
+        ],
+        axis=1,
+    )
+    dv = dot(p, gl, TN)
+    dk = dot(ds, qs[rows, :], TN)
+    dva[k] = dv if fresh else dva[k] + dv
+    dka[k] = dk if fresh else dka[k] + dk
+    return dot(ds, kbuf[0, k], NN)
 
 
 def kernel(
     n,
     len_ref, q_ref, rk_ref, rv_ref, pk_ref, pv_ref, g_ref,
     out_ref, dq_ref, drk_ref, drv_ref, dpk_ref, dpv_ref,
-    qin, gin, kbuf, ob, dqb, qs, gs, s_scr, p_scr, dkt, dvt,
-    s1, r1, s2, r2, s3, ps, pin, pown, pall,
+    qin, gin, kbuf, ob, dqb, qs, gs, de, dqa, s_scr, p_scr, dka, dva,
+    s1, r1, s2, r2, s3, ps, pin, pown, pall, len_s,
     loc, kv_send, kv_recv, qg_send, qg_recv, f_send, f_recv, o_send, o_recv,
     c_send, c_recv, x_send, x_recv, rs_send, rs_recv, ag_send, ag_recv, px_send, px_recv,
     fin,
@@ -152,6 +164,8 @@
             (pv_ref.at[:, cols], kbuf.at[1, 0, prows, :]),
         )
 
+    len_copy = pltpu.make_async_copy(len_ref, len_s, fin.at[6])
+    len_copy.start()
     kv_copies = {}
     for d in ORDER:
         kv_copies[d] = [
@@ -208,95 +222,75 @@
         wait_handed(slot, chunk, j_c, 0, core_mate)
         wait_handed(slot, chunk, 3 - j, 2, core_mate)
 
-    dkt[...] = jnp.zeros_like(dkt)
-    dvt[...] = jnp.zeros_like(dvt)
-    length = len_ref[0]
+    len_copy.wait()
+    length = len_s[0]
 
     def result_pairs(b, h):
         cols = rows_of(h, GW)
         return ((ob.at[b], out_ref.at[0, :, cols]), (dqb.at[b], dq_ref.at[0, :, cols]))
 
-    def step(i, carry):
-        d = jnp.where(i == 0, 1, jnp.where(i == 1, 3, jnp.where(i == 2, 2, 0)))
-        b = (x + 4 - d) % 4
-        for t, (src, dst) in enumerate(qg_pairs(x, b)):
-            pltpu.make_async_copy(src, dst, qg_recv.at[d, t]).wait()
-        attend_block(b, j, length, qin, gin, kbuf, ob, dqb, qs, gs, s_scr, p_scr, dkt, dvt)
-
-        @pl.when(i < 3)
-        def _():
-            for t, (src, dst) in enumerate(result_pairs(b, x)):
-                send(src, dst, o_send.at[d, t], o_recv.at[d, t], ctx=b * 4 + j).start()
-
-        return carry
-
-    lax.fori_loop(0, 4, step, 0)
-    finals = []
-    for t, (src, dst) in enumerate(result_pairs(x, x)):
-        cp = pltpu.make_async_copy(src, dst, fin.at[t])
-        cp.start()
-        finals.append(cp)
-
     def part(k, kv, jj):
-        lanes = rows_of(jj, R)
+        rows = rows_of(jj, R)
         if kv == 0:
-            return dkt[k, :, lanes].T * SCALE
-        return dvt[k, :, lanes].T
-
-    for k in range(NC):
-        for kv in range(2):
-            for zz in range(2):
-                s1[zz, kv, k] = part(k, kv, 2 * zz + 1 - core).astype(BF)
-    cp1 = send(s1, r1, c_send.at[0], c_recv.at[0], ctx=core_mate)
-    cp1.start()
-    cp1.wait_recv()
-    for k in range(NC):
-        for kv in range(2):
-            s2[kv, k] = (part(k, kv, j_z) + r1[1 - zl, kv, k].astype(F32)).astype(BF)
-    cp2 = send(s2, r2, c_send.at[1], c_recv.at[1], ctx=z_mate)
-    cp2.start()
-    cp2.wait_recv()
-
-    def total(k, kv):
-        return part(k, kv, j) + r1[zl, kv, k].astype(F32) + r2[kv, k].astype(F32)
-
-    for kv in range(2):
-        t = total(0, kv)
-        pown[kv * R : (kv + 1) * R, :] = t
-        ps[kv * R : (kv + 1) * R, :] = t.astype(BF)
+            return dka[k, rows, :] * SCALE
+        return dva[k, rows, :]
+
+    def to_core(k):
+        return send(s1.at[k], r1.at[k], c_send.at[0, k], c_recv.at[0, k], ctx=core_mate)
+
+    def to_z(k):
+        return send(s2.at[k], r2.at[k], c_send.at[1, k], c_recv.at[1, k], ctx=z_mate)
+
+    def row_pairs(at, h):
+        cols = head_cols(h)
+        return ((s3.at[at, 0], drk_ref.at[0, :, cols]), (s3.at[at, 1], drv_ref.at[0, :, cols]))
 
     def scatter(e, carry):
         to = (r + e) % n
         send(ps.at[rows_of(to, prow), :], pin.at[e], rs_send.at[e], rs_recv.at[e], resp=to).start()
         return carry
 
-    lax.fori_loop(1, n, scatter, 0)
-
-    for k in range(1, NC):
+    def give_core(k):
         for kv in range(2):
-            s3[k - 1, kv] = total(k, kv).astype(BF)
-
-    def row_pairs(at, h):
-        cols = head_cols(h)
-        return ((s3.at[at, 0], drk_ref.at[0, :, cols]), (s3.at[at, 1], drv_ref.at[0, :, cols]))
-
-    xs_copies = []
-    for d in ORDER:
-        for t, (src, dst) in enumerate(row_pairs(other(d), x)):
-            cp = send(src, dst, x_send.at[d, t], x_recv.at[d, t], ctx=other(d) * 4 + j)
-            cp.start()
-            xs_copies.append(cp)
-    for t, (src, dst) in enumerate(row_pairs(x, x)):
-        cp = pltpu.make_async_copy(src, dst, fin.at[2 + t])
-        cp.start()
-        finals.append(cp)
+            for zz in range(2):
+                s1[k, zz, kv] = part(k, kv, 2 * zz + 1 - core).astype(BF)
+        to_core(k).start()
+
+    def give_z(k):
+        to_core(k).wait_recv()
+        for kv in range(2):
+            s2[k, kv] = (part(k, kv, j_z) + r1[k, 1 - zl, kv].astype(F32)).astype(BF)
+        to_z(k).start()
+
+    def give_x(k):
+        to_z(k).wait_recv()
+        sums = [
+            part(k, kv, j) + r1[k, zl, kv].astype(F32) + r2[k, kv].astype(F32) for kv in range(2)
+        ]
+        if k == 0:
+            for kv in range(2):
+                pown[kv * R : (kv + 1) * R, :] = sums[kv]
+                ps[kv * R : (kv + 1) * R, :] = sums[kv].astype(BF)
+            lax.fori_loop(1, n, scatter, 0)
+            return
+        at = k - 1
+        for kv in range(2):
+            s3[at, kv] = sums[kv].astype(BF)
+
+        @pl.when(x == at)
+        def _():
+            for t, (src, dst) in enumerate(row_pairs(at, x)):
+                pltpu.make_async_copy(src, dst, fin.at[2 + t]).start()
+
+        @pl.when(x != at)
+        def _():
+            d = (at + 4 - x) % 4
+            for t, (src, dst) in enumerate(row_pairs(at, x)):
+                send(src, dst, x_send.at[d, t], x_recv.at[d, t], ctx=at * 4 + j).start()
 
     def gather_sum(e, acc):
         send(ps.at[rows_of(r, prow), :], pin.at[e], rs_send.at[e], rs_recv.at[e], resp=r).wait_recv()
         return acc + pin[e].astype(F32)
-
-    psum = lax.fori_loop(1, n, gather_sum, pown[rows_of(r, prow), :])
-    pall[rows_of(r, prow), :] = psum.astype(BF)
 
     def spread(e, carry):
         to = (r + e) % n
@@ -304,7 +298,70 @@
         send(view, view, ag_send.at[e], ag_recv.at[e], resp=to).start()
         return carry
 
-    lax.fori_loop(1, n, spread, 0)
+    def sum_prompt():
+        psum = lax.fori_loop(1, n, gather_sum, pown[rows_of(r, prow), :])
+        pall[rows_of(r, prow), :] = psum.astype(BF)
+        lax.fori_loop(1, n, spread, 0)
+
+    def step(i, carry):
+        d = jnp.where(i == 0, 0, jnp.where(i == 1, 1, jnp.where(i == 2, 3, 2)))
+        b = (x + 4 - d) % 4
+        for t, (src, dst) in enumerate(qg_pairs(x, b)):
+            pltpu.make_async_copy(src, dst, qg_recv.at[d, t]).wait()
+        attend_block(b, j, length, qin, gin, kbuf, ob, qs, gs, de, s_scr, p_scr)
+        src, dst = result_pairs(b, x)[0]
+
+        @pl.when(i == 0)
+        def _():
+            pltpu.make_async_copy(src, dst, fin.at[0]).start()
+
+        @pl.when(i > 0)
+        def _():
+            send(src, dst, o_send.at[d, 0], o_recv.at[d, 0], ctx=b * 4 + j).start()
+
+        return carry
+
+    lax.fori_loop(0, 4, step, 0)
+
+    def chunk_terms(k, low, fresh_dq):
+        for b in range(low, 4):
+            rows = slice(b * M, (b + 1) * M)
+            dq = grad_terms(k, rows, kbuf, qs, gs, de, p_scr, dka, dva, b == low)
+            dqa[rows, :] = dq if fresh_dq else dqa[rows, :] + dq
+
+    chunk_terms(0, 0, True)
+    give_core(0)
+    chunk_terms(4, 3, False)
+    give_core(4)
+    give_z(0)
+    chunk_terms(3, 2, False)
+    give_core(3)
+    give_z(4)
+    give_x(0)
+    chunk_terms(2, 1, False)
+    give_core(2)
+    give_z(3)
+    give_x(4)
+    sum_prompt()
+    for u, d in enumerate((2, 1, 3, 0)):
+        b = source(d)
+        rows = rows_of(b, M)
+        dq = grad_terms(1, rows, kbuf, qs, gs, de, p_scr, dka, dva, u == 0)
+        dq = ((dqa[rows, :] + dq) * SCALE).astype(BF)
+        for h in range(G):
+            dqb[b, :, h * DH : (h + 1) * DH] = dq[h * R : (h + 1) * R, :]
+        src, dst = result_pairs(b, x)[1]
+        if d:
+            send(src, dst, o_send.at[d, 1], o_recv.at[d, 1], ctx=b * 4 + j).start()
+        else:
+            pltpu.make_async_copy(src, dst, fin.at[1]).start()
+        if u == 1:
+            give_z(2)
+            give_x(3)
+    give_core(1)
+    give_x(2)
+    give_z(1)
+    finals = [pltpu.make_async_copy(src, dst, fin.at[t]) for t, (src, dst) in enumerate(result_pairs(x, x))]
 
     def collect(e, carry):
         view = pall.at[rows_of((r + n - e) % n, prow), :]
@@ -320,15 +377,19 @@
             (pall.at[rows_of(4 + at, PR), :], dpv_ref.at[:, cols]),
         )
 
+    px_copies = []
     for d in ORDER:
         for t, (src, dst) in enumerate(prompt_pairs(other(d), x)):
             cp = send(src, dst, px_send.at[d, t], px_recv.at[d, t], ctx=other(d) * 4 + j)
             cp.start()
-            xs_copies.append(cp)
+            px_copies.append(cp)
     for t, (src, dst) in enumerate(prompt_pairs(x, x)):
         cp = pltpu.make_async_copy(src, dst, fin.at[4 + t])
         cp.start()
         finals.append(cp)
+    give_x(1)
+    for t, (src, dst) in enumerate(row_pairs(x, x)):
+        finals.append(pltpu.make_async_copy(src, dst, fin.at[2 + t]))
 
     for d in ORDER:
         for t in range(2):
@@ -337,7 +398,9 @@
             cp.wait_recv()
             cp.wait_send()
             src, dst = row_pairs(x, source(d))[t]
-            send(src, dst, x_send.at[d, t], x_recv.at[d, t], ctx=c).wait_recv()
+            cp = send(src, dst, x_send.at[d, t], x_recv.at[d, t], ctx=c)
+            cp.wait_recv()
+            cp.wait_send()
             src, dst = prompt_pairs(x, source(d))[t]
             send(src, dst, px_send.at[d, t], px_recv.at[d, t], ctx=c).wait_recv()
     for cp in finals:
@@ -345,8 +408,11 @@
     for d in ORDER:
         for cp in kv_copies[d]:
             cp.wait_send()
-    for cp in qg_copies + fwd + [cp1, cp2] + xs_copies:
+    for cp in qg_copies + fwd + px_copies:
         cp.wait_send()
+    for k in range(NC):
+        to_core(k).wait_send()
+        to_z(k).wait_send()
 
     def sent(e, carry):
         send(ps.at[rows_of(r, prow), :], pin.at[e], rs_send.at[e], rs_recv.at[e], resp=r).wait_send()
@@ -357,38 +423,57 @@
     lax.fori_loop(1, n, sent, 0)
 
 
+def finish(*refs):
+    ins, outs, sems = refs[:6], refs[6:12], refs[12]
+    copies = [pltpu.make_async_copy(src, dst, sems.at[i]) for i, (src, dst) in enumerate(zip(ins, outs))]
+    for cp in copies:
+        cp.start()
+    for cp in copies:
+        cp.wait()
+
+
 def body(n, queries, resp_keys, resp_values, prompt_keys, prompt_values, out_grad, lengths):
     shape = jax.ShapeDtypeStruct
     anywhere = pl.BlockSpec(memory_space=pl.ANY)
     vmem = pltpu.VMEM
     dma = pltpu.SemaphoreType.DMA
-    return pl.pallas_call(
+    outs = (
+        shape((1, R, HQ * DH), BF),
+        shape((1, R, HQ * DH), BF),
+        shape((1, R, HK * DH), BF),
+        shape((1, R, HK * DH), BF),
+        shape((PR, HK * DH), BF),
+        shape((PR, HK * DH), BF),
+    )
+    results = pl.pallas_call(
         functools.partial(kernel, n),
-        out_shape=(
-            shape((1, R, HQ * DH), BF),
-            shape((1, R, HQ * DH), BF),
-            shape((1, R, HK * DH), BF),
-            shape((1, R, HK * DH), BF),
-            shape((PR, HK * DH), BF),
-            shape((PR, HK * DH), BF),
-        ),
-        in_specs=[pl.BlockSpec(memory_space=pltpu.SMEM)] + [anywhere] * 6,
+        out_shape=outs,
+        in_specs=[anywhere] * 7,
         out_specs=(anywhere,) * 6,
         scratch_shapes=[
             vmem((4, R, GW), BF), vmem((4, R, GW), BF), vmem((2, NC, CH, DH), BF),
-            vmem((4, R, GW), BF), vmem((4, R, GW), BF), vmem((M, DH), BF), vmem((M, DH), BF),
-            vmem((NC, M, CH), F32), vmem((NC, M, CH), BF), vmem((NC, DH, CH), F32), vmem((NC, DH, CH), F32),
-            vmem((2, 2, NC, R, DH), BF), vmem((2, 2, NC, R, DH), BF),
-            vmem((2, NC, R, DH), BF), vmem((2, NC, R, DH), BF), vmem((4, 2, R, DH), BF),
+            vmem((4, R, GW), BF), vmem((4, R, GW), BF), vmem((4 * M, DH), BF), vmem((4 * M, DH), BF),
+            vmem((4 * M, 128), F32), vmem((4 * M, DH), F32),
+            vmem((NC, M, CH), F32), vmem((NC, 4 * M, CH), BF), vmem((NC, CH, DH), F32), vmem((NC, CH, DH), F32),
+            vmem((NC, 2, 2, R, DH), BF), vmem((NC, 2, 2, R, DH), BF),
+            vmem((NC, 2, R, DH), BF), vmem((NC, 2, R, DH), BF), vmem((4, 2, R, DH), BF),
             vmem((2 * R, DH), BF), vmem((n, 256 // n, DH), BF), vmem((2 * R, DH), F32), vmem((2 * R, DH), BF),
+            pltpu.SMEM((1,), jnp.int32),
             dma((4,)), dma((3, 4)), dma((3, 4)), dma((4, 2)), dma((4, 2)), dma((5, 3)), dma((5, 3)),
-            dma((4, 2)), dma((4, 2)), dma((2,)), dma((2,)), dma((4, 2)), dma((4, 2)),
-            dma((n,)), dma((n,)), dma((n,)), dma((n,)), dma((4, 2)), dma((4, 2)), dma((6,)),
+            dma((4, 2)), dma((4, 2)), dma((2, NC)), dma((2, NC)), dma((4, 2)), dma((4, 2)),
+            dma((n,)), dma((n,)), dma((n,)), dma((n,)), dma((4, 2)), dma((4, 2)), dma((7,)),
         ],
         compiler_params=pltpu.CompilerParams(
             collective_id=0, has_side_effects=True, vmem_limit_bytes=56 << 20
         ),
     )(lengths, queries, resp_keys, resp_values, prompt_keys, prompt_values, out_grad)
+    return pl.pallas_call(
+        finish,
+        out_shape=outs,
+        in_specs=[pl.BlockSpec(memory_space=vmem)] * 6,
+        out_specs=(anywhere,) * 6,
+        scratch_shapes=[dma((6,))],
+    )(*results)
 
 
 def solution(mesh):

time: 86.4 us -> 69.7 us (0.81); the launches traced: 84.9 us -> 69.5 us
  Pallas kernels: 77.4 us -> 68.1 us
  local copies, waits for them, and re-layouts: 6.15 us -> 0 us
    pallas_call x1 -> x2, Pallas kernels: 77.4 us -> 68.1 us  [the longest x1 65.6 us: body(): pl.pallas_call(functools.partial(kernel, n), out_shape=outs, in_specs=[an...]
    unnamed x16 -> x0, local copies, waits for them, and re-layouts: 6.15 us -> none
where the time goes in v2:
time: 69.7 us; the launch traced here: 69.5 us
  Pallas kernels  68.1 us (98%)
  between operations  1.45 us (2%)
    pallas_call x1, Pallas kernels, body(): pl.pallas_call(functools.partial(kernel, n), out_shape=outs, in_specs=[an...  65.6 us
    pallas_call x1, Pallas kernels, body(): pl.pallas_call(finish, out_shape=outs, in_specs=[pl.BlockSpec(memory_spac...  2.54 us

profile of v2, /device:TPU:1, one launch (start us, length us, event | category | flops | bytes accessed | tf_op | source)
XLA Modules:
  0.0 69.5 jit_solution(13464492392157537798)
XLA Ops:
  1.3 65.6 %shard_map.118 = (bf16[1,128,2560]{2,1,0:T(8,128)(2,1)}, bf16[1,128,2560]{2,1,0:T(8,128)(2,1)}, bf16[1,128,512]{2,1,0:T(8,128)(2,1)}, bf16[1,128,512]{2,1,0:T(8,...) custom-call(s32[1]{0:T(128)S(6)} %copy.13.len_ref, bf16[1,128,2560]{2,1,0:T(8,128)(2,1)} %q_ref.1, ...), custom_call_target="tpu_custom_call" | custom-call | tf_op jit(solution)/shard_map/pallas_call | solution.py:448
  66.8 2.5 %shard_map.119 = (bf16[1,128,2560]{2,1,0:T(8,128)(2,1)}, bf16[1,128,2560]{2,1,0:T(8,128)(2,1)}, bf16[1,128,512]{2,1,0:T(8,128)(2,1)}, bf16[1,128,512]{2,1,0:T(8,...) custom-call(bf16[1,128,2560]{2,1,0:T(8,128)(2,1)} %get-tuple-element.12.refs_0_, ...), custom_call_target="tpu_custom_call" | custom-call | tf_op jit(solution)/shard_map/pallas_call | solution.py:470

commit v3 on v2

--- a/solution.py
+++ b/solution.py
@@ -39,57 +39,48 @@
 
 def attend_block(b, j, length, qin, gin, kbuf, ob, qs, gs, de, s_scr, p_scr):
     base = b * M
-    mine = rows_of(b, M)
-
-    def head(h):
-        return pl.ds(pl.multiple_of(base + h * R, R), R)
-
+    mine = slice(base, base + M)
+    last = b + 1
     for h in range(G):
-        qs[head(h), :] = qin[b, :, h * DH : (h + 1) * DH]
+        qs[base + h * R : base + (h + 1) * R, :] = qin[b, :, h * DH : (h + 1) * DH]
     q = qs[mine, :]
-
-    def scores(k, m):
+    row = lax.broadcasted_iota(jnp.int32, (R, 128), 0) + j * R
+    col = lax.broadcasted_iota(jnp.int32, (R, 128), 1)
+    m = jnp.full((M, 128), NEG, F32)
+    for k in range(last + 1):
         s = dot(q, kbuf[0, k], NT)
-        s_scr[k] = s
-        for t in range(CH // 128):
-            m = jnp.maximum(m, s[:, t * 128 : (t + 1) * 128])
-        return m
-
-    m = lax.fori_loop(0, b + 1, scores, jnp.full((M, 128), NEG, F32))
-    last = b + 1
-    s = dot(q, kbuf[0, last], NT)
-    row = lax.broadcasted_iota(jnp.int32, (R, CH), 0) + j * R
-    col = lax.broadcasted_iota(jnp.int32, (R, CH), 1)
-    s = jnp.where(jnp.concatenate([col <= row] * G, axis=0), s, NEG)
-    s_scr[last] = s
-    for t in range(CH // 128):
-        m = jnp.maximum(m, s[:, t * 128 : (t + 1) * 128])
-    top = jnp.max(m, axis=1, keepdims=True) * CEXP
-
-    def mix(k, carry):
-        o, l = carry
-        p = jnp.exp2(s_scr[k] * CEXP - top)
-        for t in range(CH // 128):
-            l = l + p[:, t * 128 : (t + 1) * 128]
-        p = p.astype(BF)
+        for t in range(0, CH, 128):
+            part = s[:, t : t + 128]
+            if k == last:
+                part = jnp.where(jnp.concatenate([col + t <= row] * G, axis=0), part, NEG)
+            s_scr[k, :, t : t + 128] = part
+            m = jnp.maximum(m, part)
+    top = jnp.broadcast_to(jnp.max(m, axis=1, keepdims=True) * CEXP, (M, 128))
+    o = jnp.zeros((M, DH), F32)
+    l = jnp.zeros((M, 128), F32)
+    for k in range(last + 1):
+        ps = []
+        for t in range(0, CH, 128):
+            p = jnp.exp2(s_scr[k, :, t : t + 128] * CEXP - top)
+            l = l + p
+            ps.append(p.astype(BF))
+        p = jnp.concatenate(ps, axis=1)
         p_scr[k, mine, :] = p
-        return o + dot(p, kbuf[1, k], NN), l
-
-    o, l = lax.fori_loop(0, b + 2, mix, (jnp.zeros((M, DH), F32), jnp.zeros((M, 128), F32)))
+        o = o + dot(p, kbuf[1, k], NN)
     rl = 1.0 / jnp.sum(l, axis=1, keepdims=True)
     token = lax.broadcasted_iota(jnp.int32, (R, 1), 0) + (4 * b + j) * R
     valid = jnp.concatenate([token < length] * G, axis=0)
     o = jnp.where(valid, o * rl, 0.0).astype(BF)
     for h in range(G):
         ob[b, :, h * DH : (h + 1) * DH] = o[h * R : (h + 1) * R, :]
-        gs[head(h), :] = gin[b, :, h * DH : (h + 1) * DH]
+        gs[base + h * R : base + (h + 1) * R, :] = gin[b, :, h * DH : (h + 1) * DH]
     gl = jnp.where(valid, gs[mine, :].astype(F32) * rl, 0.0).astype(BF)
     gs[mine, :] = gl
     delta = jnp.sum(gl.astype(F32) * o.astype(F32), axis=1, keepdims=True)
     de[mine, :] = jnp.broadcast_to(delta, (M, 128))
 
 
-def grad_terms(k, rows, kbuf, qs, gs, de, p_scr, dka, dva, fresh):
+def grad_terms(k, rows, kbuf, qs, gs, de, p_scr, dka, dva):
     gl = gs[rows, :]
     delta = de[rows, :]
     p = p_scr[k, rows, :]
@@ -101,10 +92,8 @@
         ],
         axis=1,
     )
-    dv = dot(p, gl, TN)
-    dk = dot(ds, qs[rows, :], TN)
-    dva[k] = dv if fresh else dva[k] + dv
-    dka[k] = dk if fresh else dka[k] + dk
+    dva[k] += dot(p, gl, TN)
+    dka[k] += dot(ds, qs[rows, :], TN)
     return dot(ds, kbuf[0, k], NN)
 
 
@@ -113,10 +102,10 @@
     len_ref, q_ref, rk_ref, rv_ref, pk_ref, pv_ref, g_ref,
     out_ref, dq_ref, drk_ref, drv_ref, dpk_ref, dpv_ref,
     qin, gin, kbuf, ob, dqb, qs, gs, de, dqa, s_scr, p_scr, dka, dva,
-    s1, r1, s2, r2, s3, ps, pin, pown, pall, len_s,
+    s1, r1, s2, r2, s3, ps, pin, pown, pall, pfin, len_s,
     loc, kv_send, kv_recv, qg_send, qg_recv, f_send, f_recv, o_send, o_recv,
-    c_send, c_recv, x_send, x_recv, rs_send, rs_recv, ag_send, ag_recv, px_send, px_recv,
-    fin,
+    c_send, c_recv, x_send, x_recv, rs_send, rs_recv, ag_send, ag_recv,
+    fin, lead_sem, go_sem,
 ):
     c = lax.axis_index("ctx")
     r = lax.axis_index("resp")
@@ -142,13 +131,27 @@
         )
 
     barrier = pltpu.get_barrier_semaphore()
-    for d in ORDER:
-        pl.semaphore_signal(barrier, inc=1, device_id={"ctx": other(d) * 4 + j}, device_id_type=MESH)
-    for mate in (core_mate, z_mate):
-        pl.semaphore_signal(barrier, inc=1, device_id={"ctx": mate}, device_id_type=MESH)
-    for e in range(1, n):
-        pl.semaphore_signal(barrier, inc=1, device_id={"resp": (r + e) % n}, device_id_type=MESH)
-    pl.semaphore_wait(barrier, 5 + n - 1)
+    leader = c == 0
+    near = [other(d) * 4 + j for d in ORDER] + [core_mate, z_mate]
+    for to in near:
+
+        @pl.when(to != 0)
+        def _():
+            pl.semaphore_signal(barrier, inc=1, device_id={"ctx": to}, device_id_type=MESH)
+
+    by_leader = jnp.logical_or(j == 0, jnp.logical_and(x == 0, j < 3))
+
+    @pl.when(jnp.logical_not(leader))
+    def _():
+        pl.semaphore_wait(barrier, 5)
+
+        @pl.when(by_leader)
+        def _():
+            pl.semaphore_signal(lead_sem, inc=1, device_id={"ctx": 0}, device_id_type=MESH)
+
+    @pl.when(leader)
+    def _():
+        pl.semaphore_wait(lead_sem, 5)
 
     def head_cols(h):
         return rows_of(h, DH)
@@ -215,6 +218,8 @@
     hand_on(4, 0, j, 0, core_mate)
     hand_on(4, 0, j, 1, z_mate)
     slots = [(0, 1 + x)] + [(d, 1 + source(d)) for d in ORDER] + [(4, 0)]
+    dka[...] = jnp.zeros_like(dka)
+    dva[...] = jnp.zeros_like(dva)
     for slot, chunk in slots:
         wait_handed(slot, chunk, j_z, 1, z_mate)
         hand_on(slot, chunk, j_z, 2, core_mate)
@@ -222,6 +227,22 @@
         wait_handed(slot, chunk, j_c, 0, core_mate)
         wait_handed(slot, chunk, 3 - j, 2, core_mate)
 
+    @pl.when(leader)
+    def _():
+        for e in range(1, n):
+            pl.semaphore_signal(barrier, inc=1, device_id={"resp": (r + e) % n}, device_id_type=MESH)
+
+    def meet_responses():
+        @pl.when(leader)
+        def _():
+            pl.semaphore_wait(barrier, n - 1)
+            for to in range(1, 16):
+                pl.semaphore_signal(go_sem, inc=1, device_id={"ctx": to}, device_id_type=MESH)
+
+        @pl.when(jnp.logical_not(leader))
+        def _():
+            pl.semaphore_wait(go_sem, 1)
+
     len_copy.wait()
     length = len_s[0]
 
@@ -262,53 +283,97 @@
             s2[k, kv] = (part(k, kv, j_z) + r1[k, 1 - zl, kv].astype(F32)).astype(BF)
         to_z(k).start()
 
+    def total(k, kv):
+        return part(k, kv, j) + r1[k, zl, kv].astype(F32) + r2[k, kv].astype(F32)
+
+    def give_prompt():
+        to_z(0).wait_recv()
+        for kv in range(2):
+            t = total(0, kv)
+            pown[kv * R : (kv + 1) * R, :] = t
+            ps[kv * R : (kv + 1) * R, :] = t.astype(BF)
+        meet_responses()
+        lax.fori_loop(1, n, scatter, 0)
+
     def give_x(k):
         to_z(k).wait_recv()
-        sums = [
-            part(k, kv, j) + r1[k, zl, kv].astype(F32) + r2[k, kv].astype(F32) for kv in range(2)
-        ]
-        if k == 0:
-            for kv in range(2):
-                pown[kv * R : (kv + 1) * R, :] = sums[kv]
-                ps[kv * R : (kv + 1) * R, :] = sums[kv].astype(BF)
-            lax.fori_loop(1, n, scatter, 0)
-            return
         at = k - 1
         for kv in range(2):
-            s3[at, kv] = sums[kv].astype(BF)
-
-        @pl.when(x == at)
+            s3[at, kv] = total(k, kv).astype(BF)
+
+        @pl.when(at == x)
         def _():
             for t, (src, dst) in enumerate(row_pairs(at, x)):
                 pltpu.make_async_copy(src, dst, fin.at[2 + t]).start()
 
-        @pl.when(x != at)
+        @pl.when(at != x)
         def _():
             d = (at + 4 - x) % 4
             for t, (src, dst) in enumerate(row_pairs(at, x)):
                 send(src, dst, x_send.at[d, t], x_recv.at[d, t], ctx=at * 4 + j).start()
 
+    def over(fn, low, high):
+        lax.fori_loop(low, high, lambda k, carry: (fn(k), carry)[1], 0)
+
     def gather_sum(e, acc):
         send(ps.at[rows_of(r, prow), :], pin.at[e], rs_send.at[e], rs_recv.at[e], resp=r).wait_recv()
         return acc + pin[e].astype(F32)
 
+    brows = min(PR, prow)
+    nblk = prow // brows
+    per_x = PR // brows
+
+    def piece(t):
+        g = r * nblk + t
+        kv, rest = g // (4 * per_x), g % (4 * per_x)
+        return kv, rest // per_x, rest % per_x
+
+    def piece_copy(e, t):
+        kv, at, half = piece(t)
+        src = pall.at[rows_of(r * nblk + t, brows), :]
+        dst = pfin.at[kv, rows_of(half, brows), head_cols(x)]
+        rsem = ag_recv.at[kv * per_x + half, x]
+        away = send(src, dst, ag_send.at[e, t], rsem, resp=(r + e) % n, ctx=at * 4 + j)
+        home = pltpu.make_async_copy(src, dst, rsem)
+        return away, home, jnp.logical_and(e == 0, at == x)
+
     def spread(e, carry):
-        to = (r + e) % n
-        view = pall.at[rows_of(r, prow), :]
-        send(view, view, ag_send.at[e], ag_recv.at[e], resp=to).start()
+        for t in range(nblk):
+            away, home, here = piece_copy(e, t)
+            pl.when(here)(home.start)
+            pl.when(jnp.logical_not(here))(away.start)
+        return carry
+
+    def spread_sent(e, carry):
+        for t in range(nblk):
+            away, home, here = piece_copy(e, t)
+            pl.when(jnp.logical_not(here))(away.wait_send)
+        return carry
+
+    def collect(i, carry):
+        kv, rest = i // (4 * per_x), i % (4 * per_x)
+        half, h = rest // 4, rest % 4
+        dst = pfin.at[kv, rows_of(half, brows), head_cols(h)]
+        src = pall.at[rows_of(0, brows), :]
+        pltpu.make_async_copy(src, dst, ag_recv.at[kv * per_x + half, h]).wait()
         return carry
 
     def sum_prompt():
         psum = lax.fori_loop(1, n, gather_sum, pown[rows_of(r, prow), :])
         pall[rows_of(r, prow), :] = psum.astype(BF)
-        lax.fori_loop(1, n, spread, 0)
+        lax.fori_loop(0, n, spread, 0)
 
     def step(i, carry):
         d = jnp.where(i == 0, 0, jnp.where(i == 1, 1, jnp.where(i == 2, 3, 2)))
         b = (x + 4 - d) % 4
         for t, (src, dst) in enumerate(qg_pairs(x, b)):
             pltpu.make_async_copy(src, dst, qg_recv.at[d, t]).wait()
-        attend_block(b, j, length, qin, gin, kbuf, ob, qs, gs, de, s_scr, p_scr)
+        for bb in range(4):
+
+            @pl.when(b == bb)
+            def _():
+                attend_block(bb, j, length, qin, gin, kbuf, ob, qs, gs, de, s_scr, p_scr)
+
         src, dst = result_pairs(b, x)[0]
 
         @pl.when(i == 0)
@@ -323,71 +388,95 @@
 
     lax.fori_loop(0, 4, step, 0)
 
-    def chunk_terms(k, low, fresh_dq):
-        for b in range(low, 4):
-            rows = slice(b * M, (b + 1) * M)
-            dq = grad_terms(k, rows, kbuf, qs, gs, de, p_scr, dka, dva, b == low)
-            dqa[rows, :] = dq if fresh_dq else dqa[rows, :] + dq
-
-    chunk_terms(0, 0, True)
+    def terms(k, rows):
+        return grad_terms(k, rows, kbuf, qs, gs, de, p_scr, dka, dva)
+
+    for b in range(4):
+        rows = slice(b * M, (b + 1) * M)
+        dqa[rows, :] = terms(0, rows)
     give_core(0)
-    chunk_terms(4, 3, False)
-    give_core(4)
-    give_z(0)
-    chunk_terms(3, 2, False)
-    give_core(3)
-    give_z(4)
-    give_x(0)
-    chunk_terms(2, 1, False)
-    give_core(2)
-    give_z(3)
-    give_x(4)
-    sum_prompt()
-    for u, d in enumerate((2, 1, 3, 0)):
-        b = source(d)
+
+    ends = []
+    for d in (2, 1, 3):
+        ends.append((ends[-1] if ends else 0) + source(d) + 1)
+
+    def unit(u, carry):
+        past = [u >= end for end in ends]
+        d = jnp.where(past[2], 0, jnp.where(past[1], 3, jnp.where(past[0], 1, 2)))
+        begin = jnp.where(past[2], ends[2], jnp.where(past[1], ends[1], jnp.where(past[0], ends[0], 0)))
+        b = (x + 4 - d) % 4
+        k = u - begin + 1
         rows = rows_of(b, M)
-        dq = grad_terms(1, rows, kbuf, qs, gs, de, p_scr, dka, dva, u == 0)
-        dq = ((dqa[rows, :] + dq) * SCALE).astype(BF)
-        for h in range(G):
-            dqb[b, :, h * DH : (h + 1) * DH] = dq[h * R : (h + 1) * R, :]
-        src, dst = result_pairs(b, x)[1]
-        if d:
-            send(src, dst, o_send.at[d, 1], o_recv.at[d, 1], ctx=b * 4 + j).start()
-        else:
-            pltpu.make_async_copy(src, dst, fin.at[1]).start()
-        if u == 1:
-            give_z(2)
-            give_x(3)
-    give_core(1)
-    give_x(2)
-    give_z(1)
+        dqa[rows, :] += terms(k, rows)
+        own = d == 0
+
+        @pl.when(own)
+        def _():
+            give_core(k)
+
+        @pl.when(k == b + 1)
+        def _():
+            for h in range(G):
+                dq = dqa[pl.ds(pl.multiple_of(b * M + h * R, R), R), :]
+                dqb[b, :, h * DH : (h + 1) * DH] = (dq * SCALE).astype(BF)
+            src, dst = result_pairs(b, x)[1]
+
+            @pl.when(own)
+            def _():
+                pltpu.make_async_copy(src, dst, fin.at[1]).start()
+
+            @pl.when(jnp.logical_not(own))
+            def _():
+                send(src, dst, o_send.at[d, 1], o_recv.at[d, 1], ctx=b * 4 + j).start()
+
+        @pl.when(u == 1)
+        def _():
+            give_z(0)
+
+        @pl.when(u == 4)
+        def _():
+            give_prompt()
+
+        @pl.when(u + 1 == ends[2])
+        def _():
+            over(give_core, x + 2, NC)
+
+        @pl.when(jnp.logical_and(own, k == 1))
+        def _():
+            over(give_z, x + 2, NC)
+
+        @pl.when(jnp.logical_and(own, k >= 2))
+        def _():
+            give_z(k - 1)
+
+        @pl.when(jnp.logical_and(own, k == 3))
+        def _():
+            over(give_x, x + 2, NC)
+
+        @pl.when(jnp.logical_and(own, k >= 3))
+        def _():
+            give_x(k - 2)
+
+        @pl.when(u == 8)
+        def _():
+            sum_prompt()
+
+        return carry
+
+    lax.fori_loop(0, 10, unit, 0)
+    give_z(x + 1)
+
+    @pl.when(x < 2)
+    def _():
+        over(give_x, x + 2, NC)
+
+    over(give_x, jnp.maximum(x, 1), x + 2)
     finals = [pltpu.make_async_copy(src, dst, fin.at[t]) for t, (src, dst) in enumerate(result_pairs(x, x))]
-
-    def collect(e, carry):
-        view = pall.at[rows_of((r + n - e) % n, prow), :]
-        send(view, view, ag_send.at[e], ag_recv.at[e], resp=r).wait_recv()
-        return carry
-
-    lax.fori_loop(1, n, collect, 0)
-
-    def prompt_pairs(at, h):
-        cols = head_cols(h)
-        return (
-            (pall.at[rows_of(at, PR), :], dpk_ref.at[:, cols]),
-            (pall.at[rows_of(4 + at, PR), :], dpv_ref.at[:, cols]),
-        )
-
-    px_copies = []
-    for d in ORDER:
-        for t, (src, dst) in enumerate(prompt_pairs(other(d), x)):
-            cp = send(src, dst, px_send.at[d, t], px_recv.at[d, t], ctx=other(d) * 4 + j)
-            cp.start()
-            px_copies.append(cp)
-    for t, (src, dst) in enumerate(prompt_pairs(x, x)):
-        cp = pltpu.make_async_copy(src, dst, fin.at[4 + t])
+    lax.fori_loop(0, 8 * per_x, collect, 0)
+    for kv, dst in enumerate((dpk_ref, dpv_ref)):
+        cp = pltpu.make_async_copy(pfin.at[kv], dst, fin.at[4 + kv])
         cp.start()
         finals.append(cp)
-    give_x(1)
     for t, (src, dst) in enumerate(row_pairs(x, x)):
         finals.append(pltpu.make_async_copy(src, dst, fin.at[2 + t]))
 
@@ -401,14 +490,12 @@
             cp = send(src, dst, x_send.at[d, t], x_recv.at[d, t], ctx=c)
             cp.wait_recv()
             cp.wait_send()
-            src, dst = prompt_pairs(x, source(d))[t]
-            send(src, dst, px_send.at[d, t], px_recv.at[d, t], ctx=c).wait_recv()
     for cp in finals:
         cp.wait()
     for d in ORDER:
         for cp in kv_copies[d]:
             cp.wait_send()
-    for cp in qg_copies + fwd + px_copies:
+    for cp in qg_copies + fwd:
         cp.wait_send()
     for k in range(NC):
         to_core(k).wait_send()
@@ -416,11 +503,10 @@
 
     def sent(e, carry):
         send(ps.at[rows_of(r, prow), :], pin.at[e], rs_send.at[e], rs_recv.at[e], resp=r).wait_send()
-        view = pall.at[rows_of(r, prow), :]
-        send(view, view, ag_send.at[e], ag_recv.at[e], resp=r).wait_send()
         return carry
 
     lax.fori_loop(1, n, sent, 0)
+    lax.fori_loop(0, n, spread_sent, 0)
 
 
 def finish(*refs):
@@ -458,10 +544,12 @@
             vmem((NC, 2, 2, R, DH), BF), vmem((NC, 2, 2, R, DH), BF),
             vmem((NC, 2, R, DH), BF), vmem((NC, 2, R, DH), BF), vmem((4, 2, R, DH), BF),
             vmem((2 * R, DH), BF), vmem((n, 256 // n, DH), BF), vmem((2 * R, DH), F32), vmem((2 * R, DH), BF),
+            vmem((2, PR, HK * DH), BF),
             pltpu.SMEM((1,), jnp.int32),
             dma((4,)), dma((3, 4)), dma((3, 4)), dma((4, 2)), dma((4, 2)), dma((5, 3)), dma((5, 3)),
             dma((4, 2)), dma((4, 2)), dma((2, NC)), dma((2, NC)), dma((4, 2)), dma((4, 2)),
-            dma((n,)), dma((n,)), dma((n,)), dma((n,)), dma((4, 2)), dma((4, 2)), dma((7,)),
+            dma((n,)), dma((n,)), dma((n, max(1, 8 // n))), dma((2 * max(1, n // 8), 4)), dma((7,)),
+            pltpu.SemaphoreType.REGULAR, pltpu.SemaphoreType.REGULAR,
         ],
         compiler_params=pltpu.CompilerParams(
             collective_id=0, has_side_effects=True, vmem_limit_bytes=56 << 20

time: 69.7 us -> 67.3 us (0.966); the launches traced: 69.5 us -> 66.4 us
  Pallas kernels: 68.1 us -> 64.9 us
    pallas_call x1, Pallas kernels: 65.6 us -> 62.4 us  [body(): pl.pallas_call(functools.partial(kernel, n), out_shape=outs, in_specs=[an...]
where the time goes in v3:
time: 67.3 us; the launch traced here: 66.4 us
  Pallas kernels  64.9 us (96%)
  between operations  1.45 us (2%)
    pallas_call x1, Pallas kernels, body(): pl.pallas_call(functools.partial(kernel, n), out_shape=outs, in_specs=[an...  62.4 us
    pallas_call x1, Pallas kernels, body(): pl.pallas_call(finish, out_shape=outs, in_specs=[pl.BlockSpec(memory_spac...  2.54 us

profile of v3, /device:TPU:1, one launch (start us, length us, event | category | flops | bytes accessed | tf_op | source)
XLA Modules:
  0.0 66.4 jit_solution(10244221317793972017)
XLA Ops:
  1.3 62.4 %shard_map.118 = (bf16[1,128,2560]{2,1,0:T(8,128)(2,1)}, bf16[1,128,2560]{2,1,0:T(8,128)(2,1)}, bf16[1,128,512]{2,1,0:T(8,128)(2,1)}, bf16[1,128,512]{2,1,0:T(8,...) custom-call(s32[1]{0:T(128)S(6)} %copy.13.len_ref, bf16[1,128,2560]{2,1,0:T(8,128)(2,1)} %q_ref.1, ...), custom_call_target="tpu_custom_call" | custom-call | tf_op jit(solution)/shard_map/pallas_call | solution.py:534
  63.7 2.5 %shard_map.119 = (bf16[1,128,2560]{2,1,0:T(8,128)(2,1)}, bf16[1,128,2560]{2,1,0:T(8,128)(2,1)}, bf16[1,128,512]{2,1,0:T(8,128)(2,1)}, bf16[1,128,512]{2,1,0:T(8,...) custom-call(bf16[1,128,2560]{2,1,0:T(8,128)(2,1)} %get-tuple-element.12.refs_0_, ...), custom_call_target="tpu_custom_call" | custom-call | tf_op jit(solution)/shard_map/pallas_call | solution.py:558

commit v4 on v3

--- a/solution.py
+++ b/solution.py
@@ -102,9 +102,9 @@
     len_ref, q_ref, rk_ref, rv_ref, pk_ref, pv_ref, g_ref,
     out_ref, dq_ref, drk_ref, drv_ref, dpk_ref, dpv_ref,
     qin, gin, kbuf, ob, dqb, qs, gs, de, dqa, s_scr, p_scr, dka, dva,
-    s1, r1, s2, r2, s3, ps, pin, pown, pall, pfin, len_s,
+    s1, r1, s2, r2, s3, ps, pin, pown, pz, pall, pfin, len_s,
     loc, kv_send, kv_recv, qg_send, qg_recv, f_send, f_recv, o_send, o_recv,
-    c_send, c_recv, x_send, x_recv, rs_send, rs_recv, ag_send, ag_recv,
+    c_send, c_recv, x_send, x_recv, rs_send, rs_recv, cz_send, cz_recv, ag_send, ag_recv,
     fin, lead_sem, go_sem,
 ):
     c = lax.axis_index("ctx")
@@ -116,7 +116,11 @@
     j_c = zl * 2 + (1 - core)
     j_z = (1 - zl) * 2 + core
     ORDER = (1, 3, 2)
-    prow = 256 // n
+    ny = 4 if n == 16 else 2
+    nz = n // ny
+    ry, rz = r // nz, r % nz
+    prow = 256 // ny
+    nblk = 8 // ny
 
     def other(d):
         return (x + d) % 4
@@ -266,10 +270,15 @@
         cols = head_cols(h)
         return ((s3.at[at, 0], drk_ref.at[0, :, cols]), (s3.at[at, 1], drv_ref.at[0, :, cols]))
 
-    def scatter(e, carry):
-        to = (r + e) % n
-        send(ps.at[rows_of(to, prow), :], pin.at[e], rs_send.at[e], rs_recv.at[e], resp=to).start()
-        return carry
+    def scatter_copy(e):
+        to = (ry + e) % ny
+        return send(
+            ps.at[rows_of(to, prow), :], pin.at[e], rs_send.at[e], rs_recv.at[e], resp=to * nz + rz
+        )
+
+    def cross_copy(e):
+        to = (rz + e) % nz
+        return send(pz.at[rz], pz.at[rz], cz_send.at[e], cz_recv.at[e], resp=ry * nz + to)
 
     def give_core(k):
         for kv in range(2):
@@ -293,7 +302,8 @@
             pown[kv * R : (kv + 1) * R, :] = t
             ps[kv * R : (kv + 1) * R, :] = t.astype(BF)
         meet_responses()
-        lax.fori_loop(1, n, scatter, 0)
+        for e in range(1, ny):
+            scatter_copy(e).start()
 
     def give_x(k):
         to_z(k).wait_recv()
@@ -315,53 +325,42 @@
     def over(fn, low, high):
         lax.fori_loop(low, high, lambda k, carry: (fn(k), carry)[1], 0)
 
-    def gather_sum(e, acc):
-        send(ps.at[rows_of(r, prow), :], pin.at[e], rs_send.at[e], rs_recv.at[e], resp=r).wait_recv()
-        return acc + pin[e].astype(F32)
-
-    brows = min(PR, prow)
-    nblk = prow // brows
-    per_x = PR // brows
-
-    def piece(t):
-        g = r * nblk + t
-        kv, rest = g // (4 * per_x), g % (4 * per_x)
-        return kv, rest // per_x, rest % per_x
+    def cross_prompt():
+        acc = pown[rows_of(ry, prow), :]
+        for e in range(1, ny):
+            scatter_copy(e).wait_recv()
+            acc = acc + pin[e].astype(F32)
+        pz[rz] = acc.astype(BF)
+        for e in range(1, nz):
+            cross_copy(e).start()
 
     def piece_copy(e, t):
-        kv, at, half = piece(t)
-        src = pall.at[rows_of(r * nblk + t, brows), :]
-        dst = pfin.at[kv, rows_of(half, brows), head_cols(x)]
-        rsem = ag_recv.at[kv * per_x + half, x]
-        away = send(src, dst, ag_send.at[e, t], rsem, resp=(r + e) % n, ctx=at * 4 + j)
-        home = pltpu.make_async_copy(src, dst, rsem)
-        return away, home, jnp.logical_and(e == 0, at == x)
-
-    def spread(e, carry):
-        for t in range(nblk):
-            away, home, here = piece_copy(e, t)
-            pl.when(here)(home.start)
-            pl.when(jnp.logical_not(here))(away.start)
-        return carry
-
-    def spread_sent(e, carry):
-        for t in range(nblk):
-            away, home, here = piece_copy(e, t)
-            pl.when(jnp.logical_not(here))(away.wait_send)
-        return carry
-
-    def collect(i, carry):
-        kv, rest = i // (4 * per_x), i % (4 * per_x)
-        half, h = rest // 4, rest % 4
-        dst = pfin.at[kv, rows_of(half, brows), head_cols(h)]
-        src = pall.at[rows_of(0, brows), :]
-        pltpu.make_async_copy(src, dst, ag_recv.at[kv * per_x + half, h]).wait()
-        return carry
+        g = ry * nblk + t
+        kv, at = g // 4, g % 4
+        src = pall.at[pl.ds(t * PR, PR), :]
+        dst = pfin.at[kv, :, head_cols(x)]
+        rsem = ag_recv.at[kv, x]
+        away = send(
+            src, dst, ag_send.at[e, t], rsem, resp=((ry + e) % ny) * nz + rz, ctx=at * 4 + j
+        )
+        return away, pltpu.make_async_copy(src, dst, rsem), at
 
     def sum_prompt():
-        psum = lax.fori_loop(1, n, gather_sum, pown[rows_of(r, prow), :])
-        pall[rows_of(r, prow), :] = psum.astype(BF)
-        lax.fori_loop(0, n, spread, 0)
+        for e in range(1, nz):
+            came = pz.at[(rz + nz - e) % nz]
+            send(came, came, cz_send.at[e], cz_recv.at[e], resp=r).wait_recv()
+        acc = pz[0].astype(F32)
+        for z in range(1, nz):
+            acc = acc + pz[z].astype(F32)
+        pall[...] = acc.astype(BF)
+        for e in range(ny):
+            for t in range(nblk):
+                away, home, at = piece_copy(e, t)
+                if e:
+                    away.start()
+                else:
+                    pl.when(at == x)(home.start)
+                    pl.when(at != x)(away.start)
 
     def step(i, carry):
         d = jnp.where(i == 0, 0, jnp.where(i == 1, 1, jnp.where(i == 2, 3, 2)))
@@ -429,11 +428,11 @@
             def _():
                 send(src, dst, o_send.at[d, 1], o_recv.at[d, 1], ctx=b * 4 + j).start()
 
-        @pl.when(u == 1)
+        @pl.when(u == 0)
         def _():
             give_z(0)
 
-        @pl.when(u == 4)
+        @pl.when(u == 3)
         def _():
             give_prompt()
 
@@ -457,9 +456,9 @@
         def _():
             give_x(k - 2)
 
-        @pl.when(u == 8)
-        def _():
-            sum_prompt()
+        @pl.when(u == 6)
+        def _():
+            cross_prompt()
 
         return carry
 
@@ -470,9 +469,13 @@
     def _():
         over(give_x, x + 2, NC)
 
+    sum_prompt()
     over(give_x, jnp.maximum(x, 1), x + 2)
     finals = [pltpu.make_async_copy(src, dst, fin.at[t]) for t, (src, dst) in enumerate(result_pairs(x, x))]
-    lax.fori_loop(0, 8 * per_x, collect, 0)
+    for kv in range(2):
+        for h in range(4):
+            src, dst = pall.at[pl.ds(0, PR), :], pfin.at[kv, :, head_cols(h)]
+            pltpu.make_async_copy(src, dst, ag_recv.at[kv, h]).wait()
     for kv, dst in enumerate((dpk_ref, dpv_ref)):
         cp = pltpu.make_async_copy(pfin.at[kv], dst, fin.at[4 + kv])
         cp.start()
@@ -501,12 +504,17 @@
         to_core(k).wait_send()
         to_z(k).wait_send()
 
-    def sent(e, carry):
-        send(ps.at[rows_of(r, prow), :], pin.at[e], rs_send.at[e], rs_recv.at[e], resp=r).wait_send()
-        return carry
-
-    lax.fori_loop(1, n, sent, 0)
-    lax.fori_loop(0, n, spread_sent, 0)
+    for e in range(1, ny):
+        scatter_copy(e).wait_send()
+    for e in range(1, nz):
+        cross_copy(e).wait_send()
+    for e in range(ny):
+        for t in range(nblk):
+            away, home, at = piece_copy(e, t)
+            if e:
+                away.wait_send()
+            else:
+                pl.when(at != x)(away.wait_send)
 
 
 def finish(*refs):
@@ -520,6 +528,7 @@
 
 def body(n, queries, resp_keys, resp_values, prompt_keys, prompt_values, out_grad, lengths):
     shape = jax.ShapeDtypeStruct
+    ny = 4 if n == 16 else 2
     anywhere = pl.BlockSpec(memory_space=pl.ANY)
     vmem = pltpu.VMEM
     dma = pltpu.SemaphoreType.DMA
@@ -543,12 +552,13 @@
             vmem((NC, M, CH), F32), vmem((NC, 4 * M, CH), BF), vmem((NC, CH, DH), F32), vmem((NC, CH, DH), F32),
             vmem((NC, 2, 2, R, DH), BF), vmem((NC, 2, 2, R, DH), BF),
             vmem((NC, 2, R, DH), BF), vmem((NC, 2, R, DH), BF), vmem((4, 2, R, DH), BF),
-            vmem((2 * R, DH), BF), vmem((n, 256 // n, DH), BF), vmem((2 * R, DH), F32), vmem((2 * R, DH), BF),
+            vmem((2 * R, DH), BF), vmem((ny, 256 // ny, DH), BF), vmem((2 * R, DH), F32),
+            vmem((n // ny, 256 // ny, DH), BF), vmem((256 // ny, DH), BF),
             vmem((2, PR, HK * DH), BF),
             pltpu.SMEM((1,), jnp.int32),
             dma((4,)), dma((3, 4)), dma((3, 4)), dma((4, 2)), dma((4, 2)), dma((5, 3)), dma((5, 3)),
             dma((4, 2)), dma((4, 2)), dma((2, NC)), dma((2, NC)), dma((4, 2)), dma((4, 2)),
-            dma((n,)), dma((n,)), dma((n, max(1, 8 // n))), dma((2 * max(1, n // 8), 4)), dma((7,)),
+            dma((ny,)), dma((ny,)), dma((n // ny,)), dma((n // ny,)), dma((ny, 8 // ny)), dma((2, 4)), dma((7,)),
             pltpu.SemaphoreType.REGULAR, pltpu.SemaphoreType.REGULAR,
         ],
         compiler_params=pltpu.CompilerParams(

time: 67.3 us -> 63.9 us (0.949)
  Pallas kernels: 64.9 us -> 62.2 us
    pallas_call x1, Pallas kernels: 62.4 us -> 59.6 us  [body(): pl.pallas_call(functools.partial(kernel, n), out_shape=outs, in_specs=[an...]
where the time goes in v4:
time: 63.9 us; the launch traced here: 63.6 us
  Pallas kernels  62.2 us (97%)
  between operations  1.45 us (2%)
    pallas_call x1, Pallas kernels, body(): pl.pallas_call(functools.partial(kernel, n), out_shape=outs, in_specs=[an...  59.6 us
    pallas_call x1, Pallas kernels, body(): pl.pallas_call(finish, out_shape=outs, in_specs=[pl.BlockSpec(memory_spac...  2.54 us

profile of v4, /device:TPU:1, one launch (start us, length us, event | category | flops | bytes accessed | tf_op | source)
XLA Modules:
  0.0 63.6 jit_solution(2618564789323625319)
XLA Ops:
  1.3 59.6 %shard_map.118 = (bf16[1,128,2560]{2,1,0:T(8,128)(2,1)}, bf16[1,128,2560]{2,1,0:T(8,128)(2,1)}, bf16[1,128,512]{2,1,0:T(8,128)(2,1)}, bf16[1,128,512]{2,1,0:T(8,...) custom-call(s32[1]{0:T(128)S(6)} %copy.13.len_ref, bf16[1,128,2560]{2,1,0:T(8,128)(2,1)} %q_ref.1, ...), custom_call_target="tpu_custom_call" | custom-call | tf_op jit(solution)/shard_map/pallas_call | solution.py:543
  60.9 2.5 %shard_map.119 = (bf16[1,128,2560]{2,1,0:T(8,128)(2,1)}, bf16[1,128,2560]{2,1,0:T(8,128)(2,1)}, bf16[1,128,512]{2,1,0:T(8,128)(2,1)}, bf16[1,128,512]{2,1,0:T(8,...) custom-call(bf16[1,128,2560]{2,1,0:T(8,128)(2,1)} %get-tuple-element.12.refs_0_, ...), custom_call_target="tpu_custom_call" | custom-call | tf_op jit(solution)/shard_map/pallas_call | solution.py:568

commit v5 on v4

--- a/solution.py
+++ b/solution.py
@@ -465,11 +465,12 @@
     lax.fori_loop(0, 10, unit, 0)
     give_z(x + 1)
 
+    sum_prompt()
+
     @pl.when(x < 2)
     def _():
         over(give_x, x + 2, NC)
 
-    sum_prompt()
     over(give_x, jnp.maximum(x, 1), x + 2)
     finals = [pltpu.make_async_copy(src, dst, fin.at[t]) for t, (src, dst) in enumerate(result_pairs(x, x))]
     for kv in range(2):

time: 63.9 us -> 63.7 us (level)
  no operation moved by 1% of the time
where the time goes in v5:
time: 63.7 us; the launch traced here: 63.6 us
  Pallas kernels  62.1 us (97%)
  between operations  1.45 us (2%)
    pallas_call x1, Pallas kernels, body(): pl.pallas_call(functools.partial(kernel, n), out_shape=outs, in_specs=[an...  59.6 us
    pallas_call x1, Pallas kernels, body(): pl.pallas_call(finish, out_shape=outs, in_specs=[pl.BlockSpec(memory_spac...  2.54 us

profile of v5, /device:TPU:1, one launch (start us, length us, event | category | flops | bytes accessed | tf_op | source)
XLA Modules:
  0.0 63.6 jit_solution(6516913434822240773)
XLA Ops:
  1.3 59.6 %shard_map.118 = (bf16[1,128,2560]{2,1,0:T(8,128)(2,1)}, bf16[1,128,2560]{2,1,0:T(8,128)(2,1)}, bf16[1,128,512]{2,1,0:T(8,128)(2,1)}, bf16[1,128,512]{2,1,0:T(8,...) custom-call(s32[1]{0:T(128)S(6)} %copy.13.len_ref, bf16[1,128,2560]{2,1,0:T(8,128)(2,1)} %q_ref.1, ...), custom_call_target="tpu_custom_call" | custom-call | tf_op jit(solution)/shard_map/pallas_call | solution.py:544
  60.9 2.5 %shard_map.119 = (bf16[1,128,2560]{2,1,0:T(8,128)(2,1)}, bf16[1,128,2560]{2,1,0:T(8,128)(2,1)}, bf16[1,128,512]{2,1,0:T(8,128)(2,1)}, bf16[1,128,512]{2,1,0:T(8,...) custom-call(bf16[1,128,2560]{2,1,0:T(8,128)(2,1)} %get-tuple-element.12.refs_0_, ...), custom_call_target="tpu_custom_call" | custom-call | tf_op jit(solution)/shard_map/pallas_call | solution.py:569
